TPU v7x, 32 devices: a whole 2x2x4 slice. The times are simulated.
32 devices in a mesh: dp: 8 (over z, x), tensor: 4 (over y, core).
Axes of the slice: x: 2, y: 2, z: 4, core: 2. Of those that a mesh axis runs over, the one named last changes fastest.
Arguments:
- series: bfloat16 [32, 864, 96], P('dp', 'tensor'), may hold values from -6 to 6
- embed_weight: bfloat16 [96, 512], replicated, may hold values from -0.625 to 0.625
- embed_bias: float32 [512], replicated, may hold values from -3 to 3
- query_weight: bfloat16 [512, 512], replicated, may hold values from -0.25 to 0.25
- query_bias: float32 [512], replicated, may hold values from -1.75 to 1.75
- key_weight: bfloat16 [512, 512], replicated, may hold values from -0.25 to 0.25
- value_weight: bfloat16 [512, 512], replicated, may hold values from -0.25 to 0.25
- value_bias: float32 [512], replicated, may hold values from -0.1875 to 0.1875
- out_weight: bfloat16 [512, 512], replicated, may hold values from -3 to 3
- out_bias: float32 [512], replicated, may hold values from -1.75 to 1.75
- first_gain: float32 [512], replicated, may hold values from 0.25 to 1.75
- first_shift: float32 [512], replicated, may hold values from -1.75 to 1.75
- up_weight: bfloat16 [2048, 512], P('tensor'), may hold values from -0.25 to 0.25
- up_bias: bfloat16 [2048], P('tensor'), may hold values from -1.75 to 1.75
- down_weight: bfloat16 [2048, 512], P('tensor'), may hold values from -0.125 to 0.125
- down_bias: float32 [512], replicated, may hold values from -1.75 to 1.75
- second_gain: float32 [512], replicated, may hold values from 0.25 to 1.75
- second_shift: float32 [512], replicated, may hold values from -1.75 to 1.75
- cotangent: bfloat16 [32, 864, 512], P('dp', 'tensor'), may hold values from -8 to 8
Outputs:
- mixed_out: bfloat16 [32, 864, 512], P('dp', 'tensor')
- series_grad: bfloat16 [32, 864, 96], P('dp', 'tensor')
- embed_weight_grad: float32 [96, 512], replicated
- embed_bias_grad: float32 [512], replicated
- query_weight_grad: float32 [512, 512], replicated
- query_bias_grad: float32 [512], replicated
- key_weight_grad: float32 [512, 512], replicated
- value_weight_grad: float32 [512, 512], replicated
- value_bias_grad: float32 [512], replicated
- out_weight_grad: float32 [512, 512], replicated
- out_bias_grad: float32 [512], replicated
- first_gain_grad: float32 [512], replicated
- first_shift_grad: float32 [512], replicated
- up_weight_grad: float32 [2048, 512], P('tensor', 'dp')
- up_bias_grad: float32 [2048], replicated
- down_weight_grad: float32 [2048, 512], P('tensor', 'dp')
- down_bias_grad: float32 [512], replicated
- second_gain_grad: float32 [512], replicated
- second_shift_grad: float32 [512], replicated
All inputs are finite; a program needn't handle non-finite values.
Results may differ from a plain program's by a relative error of at most 0.02.
Values may be sent and summed in bfloat16 or wider, within the bound.
A program may use at most 128 MiB of HBM per device.

v0:
```python
import jax
import jax.numpy as jnp
from jax import lax
from jax.sharding import PartitionSpec as P

HEADS = 8
FF = 2048


EPSILON = 1e-05


def layer_norm(row_values, norm_gain, norm_shift):
    average = jnp.mean(row_values, axis=-1, keepdims=True)
    centred = row_values - average
    variance = jnp.mean(centred * centred, axis=-1, keepdims=True)
    inverse = lax.rsqrt(variance + EPSILON)
    normed = centred * inverse
    return (normed * norm_gain + norm_shift, normed, inverse)


def layer_norm_back(upstream, normed, inverse, norm_gain):
    scaled = upstream * norm_gain
    first_term = jnp.mean(scaled, axis=-1, keepdims=True)
    second_term = jnp.mean(scaled * normed, axis=-1, keepdims=True)
    grad_input = inverse * (scaled - first_term - normed * second_term)
    return (grad_input, jnp.sum(upstream * normed, axis=0), jnp.sum(upstream, axis=0))


def contract_rows(left_side, right_side):
    return lax.dot_general(
        left_side, right_side, (((0,), (0,)), ((), ())), preferred_element_type=jnp.float32
    )


def contract_last(left_side, right_side):
    return lax.dot_general(
        left_side, right_side, (((1,), (1,)), ((), ())), preferred_element_type=jnp.float32
    )


def attend(queries, keys_all, values_all, factor):
    scores = (
        jnp.einsum("qhe,khe->hqk", queries, keys_all, preferred_element_type=jnp.float32) * factor
    )
    row_top = jnp.max(scores, axis=-1, keepdims=True)
    exponent = jnp.exp(scores - row_top)
    row_total = jnp.sum(exponent, axis=-1, keepdims=True)
    probability = (exponent / row_total).astype(jnp.bfloat16)
    mixed = jnp.einsum("hqk,khe->qhe", probability, values_all, preferred_element_type=jnp.float32)
    return (mixed, row_top + jnp.log(row_total))


def attend_back(queries, keys_all, values_all, logsum, grad_mixed, factor):
    scores = (
        jnp.einsum("qhe,khe->hqk", queries, keys_all, preferred_element_type=jnp.float32) * factor
    )
    probability = jnp.exp(scores - logsum)
    grad_values = jnp.einsum(
        "hqk,qhe->khe",
        probability.astype(jnp.bfloat16),
        grad_mixed,
        preferred_element_type=jnp.float32,
    )
    grad_probability = jnp.einsum(
        "qhe,khe->hqk", grad_mixed, values_all, preferred_element_type=jnp.float32
    )
    centre = jnp.sum(probability * grad_probability, axis=-1, keepdims=True)
    grad_scores = (probability * (grad_probability - centre)).astype(jnp.bfloat16)
    grad_queries = (
        jnp.einsum("hqk,khe->qhe", grad_scores, keys_all, preferred_element_type=jnp.float32)
        * factor
    )
    grad_keys = (
        jnp.einsum("hqk,qhe->khe", grad_scores, queries, preferred_element_type=jnp.float32)
        * factor
    )
    return (grad_queries, grad_keys, grad_values)


def body(
    series,
    embed_weight,
    embed_bias,
    query_weight,
    query_bias,
    key_weight,
    value_weight,
    value_bias,
    out_weight,
    out_bias,
    first_gain,
    first_shift,
    up_weight,
    up_bias,
    down_weight,
    down_bias,
    second_gain,
    second_shift,
    cotangent,
):
    windows, own_rows, lookback = series.shape
    model_width = embed_weight.shape[1]
    head_size = model_width // HEADS
    factor = head_size ** (-0.5)
    total_rows = windows * own_rows
    flat_series = series.reshape(total_rows, lookback)
    embedded = jnp.dot(flat_series, embed_weight, preferred_element_type=jnp.float32) + embed_bias
    embedded_low = embedded.astype(jnp.bfloat16)
    queries = (
        jnp.dot(embedded_low, query_weight, preferred_element_type=jnp.float32) + query_bias
    ).astype(jnp.bfloat16)
    keys_own = jnp.dot(embedded_low, key_weight, preferred_element_type=jnp.float32).astype(
        jnp.bfloat16
    )
    values_own = (
        jnp.dot(embedded_low, value_weight, preferred_element_type=jnp.float32) + value_bias
    ).astype(jnp.bfloat16)
    queries_split = queries.reshape(windows, own_rows, HEADS, head_size)

    def forward_window(window_inputs):
        return attend(window_inputs[0], window_inputs[1], window_inputs[2], factor)

    def backward_window(window_inputs):
        return attend_back(
            window_inputs[0],
            window_inputs[1],
            window_inputs[2],
            window_inputs[3],
            window_inputs[4],
            factor,
        )

    key_value = jnp.concatenate([keys_own, values_own], axis=-1).reshape(
        windows, own_rows, 2 * model_width
    )
    key_value_all = lax.all_gather(key_value, "tensor", axis=1, tiled=True)
    variates = key_value_all.shape[1]
    keys_all = key_value_all[..., :model_width].reshape(windows, variates, HEADS, head_size)
    values_all = key_value_all[..., model_width:].reshape(windows, variates, HEADS, head_size)
    mixed, logsum = lax.map(forward_window, (queries_split, keys_all, values_all))
    mixed_low = mixed.reshape(total_rows, model_width).astype(jnp.bfloat16)
    attended = jnp.dot(mixed_low, out_weight, preferred_element_type=jnp.float32) + out_bias
    first_out, first_normed, first_inverse = layer_norm(
        embedded + attended, first_gain, first_shift
    )
    first_low = first_out.astype(jnp.bfloat16)
    gathered = lax.all_gather(
        first_low.reshape(windows, own_rows, model_width), "tensor", axis=1, tiled=True
    )
    pre_hidden = jnp.einsum(
        "wvd,fd->wvf", gathered, up_weight, preferred_element_type=jnp.float32
    ) + up_bias.astype(jnp.float32)
    hidden_low = jax.nn.gelu(pre_hidden).astype(jnp.bfloat16)
    partial_value = jnp.einsum(
        "wvf,fd->wvd", hidden_low, down_weight, preferred_element_type=jnp.float32
    )
    branch_sum = (
        lax.psum_scatter(
            partial_value.astype(jnp.bfloat16), "tensor", scatter_dimension=1, tiled=True
        )
        .astype(jnp.float32)
        .reshape(total_rows, model_width)
    )
    branch = branch_sum + down_bias
    second_out, second_normed, second_inverse = layer_norm(
        first_out + branch, second_gain, second_shift
    )
    result = second_out.astype(jnp.bfloat16).reshape(windows, own_rows, model_width)
    upstream = cotangent.reshape(total_rows, model_width).astype(jnp.float32)
    grad_second_in, second_gain_grad, second_shift_grad = layer_norm_back(
        upstream, second_normed, second_inverse, second_gain
    )
    grad_branch = grad_second_in.astype(jnp.bfloat16)
    down_bias_grad = jnp.sum(grad_branch, axis=0, dtype=jnp.float32)
    _, slope_back = jax.vjp(jax.nn.gelu, pre_hidden)
    grad_gathered = lax.all_gather(
        grad_branch.reshape(windows, own_rows, model_width), "tensor", axis=1, tiled=True
    )
    grad_hidden = jnp.einsum(
        "wvd,fd->wvf", grad_gathered, down_weight, preferred_element_type=jnp.float32
    )
    grad_pre = slope_back(grad_hidden)[0].astype(jnp.bfloat16)
    down_share = jnp.einsum(
        "wvf,wvd->fd", hidden_low, grad_gathered, preferred_element_type=jnp.float32
    )
    up_share = jnp.einsum("wvf,wvd->fd", grad_pre, gathered, preferred_element_type=jnp.float32)
    share_size = up_weight.shape[0]
    bias_share = jnp.sum(grad_pre, axis=(0, 1), dtype=jnp.float32)
    offset = lax.axis_index("tensor") * share_size
    up_bias_grad = lax.dynamic_update_slice(jnp.zeros((FF,), jnp.float32), bias_share, (offset,))
    grad_first_part = jnp.einsum(
        "wvf,fd->wvd", grad_pre, up_weight, preferred_element_type=jnp.float32
    )
    grad_first_ffn = (
        lax.psum_scatter(
            grad_first_part.astype(jnp.bfloat16), "tensor", scatter_dimension=1, tiled=True
        )
        .astype(jnp.float32)
        .reshape(total_rows, model_width)
    )
    up_weight_grad, down_weight_grad = (
        lax.psum_scatter(up_share, "dp", scatter_dimension=1, tiled=True),
        lax.psum_scatter(down_share, "dp", scatter_dimension=1, tiled=True),
    )
    grad_first_out = grad_second_in + grad_first_ffn
    grad_first_in, first_gain_grad, first_shift_grad = layer_norm_back(
        grad_first_out, first_normed, first_inverse, first_gain
    )
    grad_attended = grad_first_in.astype(jnp.bfloat16)
    out_bias_grad = jnp.sum(grad_attended, axis=0, dtype=jnp.float32)
    out_weight_grad = contract_rows(mixed_low, grad_attended)
    grad_mixed = contract_last(grad_attended, out_weight).astype(jnp.bfloat16)
    grad_mixed_split = grad_mixed.reshape(windows, own_rows, HEADS, head_size)
    grad_queries, grad_keys_part, grad_values_part = lax.map(
        backward_window, (queries_split, keys_all, values_all, logsum, grad_mixed_split)
    )
    grad_key_value_part = jnp.concatenate(
        [
            grad_keys_part.reshape(windows, variates, model_width),
            grad_values_part.reshape(windows, variates, model_width),
        ],
        axis=-1,
    )
    grad_key_value = lax.psum_scatter(
        grad_key_value_part.astype(jnp.bfloat16), "tensor", scatter_dimension=1, tiled=True
    ).astype(jnp.float32)
    grad_keys = (
        grad_key_value[..., :model_width].reshape(total_rows, model_width).astype(jnp.bfloat16)
    )
    grad_values = (
        grad_key_value[..., model_width:].reshape(total_rows, model_width).astype(jnp.bfloat16)
    )
    grad_queries_low = grad_queries.reshape(total_rows, model_width).astype(jnp.bfloat16)
    query_weight_grad = contract_rows(embedded_low, grad_queries_low)
    query_bias_grad = jnp.sum(grad_queries_low, axis=0, dtype=jnp.float32)
    key_weight_grad = contract_rows(embedded_low, grad_keys)
    value_weight_grad = contract_rows(embedded_low, grad_values)
    value_bias_grad = jnp.sum(grad_values, axis=0, dtype=jnp.float32)
    grad_embedded_part = (
        contract_last(grad_queries_low, query_weight)
        + contract_last(grad_keys, key_weight)
        + contract_last(grad_values, value_weight)
    )
    grad_embedded = (grad_first_in + grad_embedded_part).astype(jnp.bfloat16)
    embed_weight_grad = contract_rows(flat_series, grad_embedded)
    embed_bias_grad = jnp.sum(grad_embedded, axis=0, dtype=jnp.float32)
    series_grad = (
        contract_last(grad_embedded, embed_weight)
        .astype(jnp.bfloat16)
        .reshape(windows, own_rows, lookback)
    )
    summed = lax.psum(
        (
            embed_weight_grad,
            embed_bias_grad,
            query_weight_grad,
            query_bias_grad,
            key_weight_grad,
            value_weight_grad,
            value_bias_grad,
            out_weight_grad,
            out_bias_grad,
            first_gain_grad,
            first_shift_grad,
            up_bias_grad,
            down_bias_grad,
            second_gain_grad,
            second_shift_grad,
        ),
        ("dp", "tensor"),
    )
    return (
        result,
        series_grad,
        summed[0],
        summed[1],
        summed[2],
        summed[3],
        summed[4],
        summed[5],
        summed[6],
        summed[7],
        summed[8],
        summed[9],
        summed[10],
        up_weight_grad,
        summed[11],
        down_weight_grad,
        summed[12],
        summed[13],
        summed[14],
    )


def solution(mesh):
    return jax.shard_map(
        body,
        mesh=mesh,
        in_specs=(
            P("dp", "tensor", None),
            P(),
            P(),
            P(),
            P(),
            P(),
            P(),
            P(),
            P(),
            P(),
            P(),
            P(),
            P("tensor", None),
            P("tensor"),
            P("tensor", None),
            P(),
            P(),
            P(),
            P("dp", "tensor", None),
        ),
        out_specs=(
            P("dp", "tensor", None),
            P("dp", "tensor", None),
            P(),
            P(),
            P(),
            P(),
            P(),
            P(),
            P(),
            P(),
            P(),
            P(),
            P(),
            P("tensor", "dp"),
            P(),
            P("tensor", "dp"),
            P(),
            P(),
            P(),
        ),
        check_vma=False,
    )
```

profile of v0, /device:TPU:0, one launch (start us, length us, event | category | flops | bytes accessed | tf_op | source)
XLA Modules:
  0.0 837.1 jit_solution(2902415010952030721)
XLA Ops:
  19.4 48.5 %all-gather.4.cloned.1.call-done = bf16[4,864,1024]{2,1,0:T(8,128)(2,1)} async-done(((bf16[4,216,1024]{2,1,0:T(8,128)(2,1)}), bf16[4,864,1024]{2,1,0:T(8,128)(2,1)}) %all-gather.4.cloned.1.call-update) | async-done | bytes 7077904 | tf_op jit(solution)/shard_map/all_gather | solution.py:137
  67.9 6.5 fusion.67
  74.3 5.9 copy.73
  80.3 6.0 copy.71
  86.4 26.3 %while.26 = (s32[]{:T(128)}, bf16[4,216,8,64]{1,3,2,0:T(8,128)(2,1)S(1)}, f32[4,8,216,1]{2,1,3,0:T(8,128)S(1)}, bf16[4,864,8,64]{1,3,2,0:T(8,128)(2,1)}, bf16[4,...) while((s32[]{:T(128)}, bf16[4,216,8,64]{1,3,2,0:T(8,128)(2,1)S(1)}, ...), condition=%wide.region_3.4_spmd, body=%wide.region_0.3_spmd.sunk | while | flops 395641152 | bytes 20822360 | solution.py:141
  114.5 3.1 convert_element_type.118
  122.3 30.7 %all-gather.6.cloned.1.call-done = bf16[4,864,512]{2,1,0:T(8,128)(2,1)} async-done(((bf16[4,216,512]{2,1,0:T(8,128)(2,1)}), bf16[4,864,512]{2,1,0:T(8,128)(2,1)}) %all-gather.6.cloned.1.call-update) | async-done | bytes 3538960 | tf_op jit(solution)/shard_map/all_gather | solution.py:148
  153.0 4.3 fusion.59
  157.3 2.9 copy-done.14
  160.2 3.1 convolution_convert_fusion.1
  172.0 37.6 %reduce-scatter.13.cloned.1.call-done = bf16[216,2048]{1,0:T(8,128)(2,1)} async-done(((bf16[864,2048]{1,0:T(8,128)(2,1)}), bf16[216,2048]{1,0:T(8,128)(2,1)}) %reduce-scatter.13.cloned.1.call-update) | async-done | bytes 884752
  209.5 3.2 reshape.211
  220.5 30.5 %all-gather.8.cloned.1.call-done = bf16[4,864,512]{2,1,0:T(8,128)(2,1)} async-done(((bf16[4,216,512]{2,1,0:T(8,128)(2,1)}), bf16[4,864,512]{2,1,0:T(8,128)(2,1)}) %all-gather.8.cloned.1.call-update) | async-done | bytes 3538960 | tf_op jit(solution)/shard_map/all_gather | solution.py:177
  251.0 9.0 %convert_reduce_fusion = (f32[512]{0:T(512)S(1)}, bf16[4,864,512]{2,1,0:T(8,128)(2,1)S(1)}) fusion(f32[4,864,512]{2,1,0:T(8,128)} %copy-done.14, f32[512]{0:T(512)S(1)} %convert_element_type.120, bf16[4,864,512]{2,1,0:T(8,128)(2,1)} %all-gather.8.cloned.1.call-done, bf16[512,512]{1,0:T(8,128)(2,1)S(1)} %copy-done), kind=kOutput, calls=%fused_computation.63 | convolution fusion | flops 1852636672 | bytes 14684160 | tf_op jit(solution)/shard_map/wvd,fd->wvf/dot_general | solution.py:180
  269.7 40.3 %reduce-scatter.15.cloned.1.call-done = bf16[216,2048]{1,0:T(8,128)(2,1)} async-done(((bf16[864,2048]{1,0:T(8,128)(2,1)}), bf16[216,2048]{1,0:T(8,128)(2,1)}) %reduce-scatter.15.cloned.1.call-update) | async-done | bytes 884752
  310.0 3.2 reshape.213
  325.1 57.9 %while.27 = (s32[]{:T(128)}, bf16[4,216,8,64]{1,3,2,0:T(8,128)(2,1)}, bf16[4,864,8,64]{1,3,2,0:T(8,128)(2,1)}, bf16[4,864,8,64]{1,3,2,0:T(8,128)(2,1)}, bf16[4,8...) while((s32[]{:T(128)}, ...), condition=%wide.region_16.17_spmd, body=%wide.region_14.16_spmd.sunk | while | flops 973982016 | bytes 117206048 | solution.py:215
  329.1 3.6 multiply_reduce_fusion.11
  343.6 3.6 multiply_reduce_fusion.11
  358.1 3.6 multiply_reduce_fusion.11
  372.5 3.6 multiply_reduce_fusion.11
  383.0 6.7 pad_maximum_fusion
  389.8 13.1 %copy.80 = bf16[4,864,1024]{2,0,1:T(4,128)(2,1)} copy(bf16[4,864,1024]{1,2,0:T(8,128)(2,1)} %pad_maximum_fusion) | data formatting | bytes 14155776 | tf_op jit(solution)/shard_map/concatenate | solution.py:218
  403.1 6.2 convolution_bitcast_fusion.1
  410.7 8.4 convolution_bitcast_fusion
  421.7 3.3 fusion.69
  425.0 3.2 fusion.71
  429.9 105.5 %all-reduce.6.cloned.1.call-done = bf16[4,864,1024]{2,0,1:T(4,128)(2,1)} async-done(((bf16[4,864,1024]{2,0,1:T(4,128)(2,1)}), bf16[4,864,1024]{2,0,1:T(4,128)(2,1)}) %all-reduce.6.cloned.1.call-update) | async-done | bytes 7077904
  548.1 40.5 %all-reduce.1 = (f32[512]{0:T(512)}, f32[512]{0:T(512)}, f32[512]{0:T(512)}, f32[512]{0:T(512)}, f32[512]{0:T(512)}, /*index=5*/f32[512]{0:T(512)}, f32[2048]{0:...) all-reduce(f32[512]{0:T(512)S(1)} %get-tuple-element.315, ...), channel_id=1, replica_groups=mesh['dp'=8,'tensor'=4] {'dp','tensor'}, use_global_device_ids=true, to_apply=%region_20.21 | all-reduce | flops 6656 | bytes 53248 | tf_op jit(solution)/shard_map/psum | solution.py:253
  588.6 14.5 %reduce-scatter.9.cloned.1.call-done = f32[512,64]{0,1:T(8,128)} async-done(((f32[512,512]{0,1:T(8,128)}), f32[512,64]{0,1:T(8,128)}) %reduce-scatter.9.cloned.1.call-update) | async-done | bytes 131088 | tf_op jit(solution)/shard_map/reduce_scatter | solution.py:203
  603.1 66.9 %reduce-scatter.11.cloned.1.call-done = f32[512,64]{0,1:T(8,128)} async-done(((f32[512,512]{0,1:T(8,128)}), f32[512,64]{0,1:T(8,128)}) %reduce-scatter.11.cloned.1.call-update) | async-done | bytes 131088 | tf_op jit(solution)/shard_map/reduce_scatter | solution.py:204
  670.0 151.9 %all-reduce.8.cloned.1.call-done = (f32[96,512]{1,0:T(8,128)}, f32[512,512]{1,0:T(8,128)}, f32[512,512]{1,0:T(8,128)}, f32[512,512]{1,0:T(8,128)}, f32[512,512]{1,0:T(8,128)}) async-done(((f32[96,512]{1,0:T(8,128)}, f32[512,512]{1,0:T(8,128)}, f32[512,512]{1,0:T(8,128)}, f32[512,512]{1,0:T(8,128)}, f32[512,512]{1,0:T(8,128)}), (f32[96,512]{1,0:T(8,128)}, f32[512,512]{1,0:T(8,128)}, f32[512,512]{1,0:T(8,128)}, ...) | async-done | bytes 4390928 | tf_op jit(solution)/shard_map/psum | solution.py:253
  (261 shorter events, 152.2 us)
Async XLA Ops:
  7.2 153.0 %copy-start = (bf16[512,512]{1,0:T(8,128)(2,1)S(1)}, bf16[512,512]{1,0:T(8,128)(2,1)}, u32[]{:S(2)}) copy-start(bf16[512,512]{1,0:T(8,128)(2,1)} %param.37) | copy-start | bytes 1572868
  7.2 4.1 copy-start.30
  7.2 4.7 copy-start.32
  7.2 4.7 copy-start.44
  7.2 60.6 %all-gather.4.cloned.1.call-start = ((), (), s32[]{:S(2)}) async-start(), calls=%async_computation.4 | async-start | bytes 8847360 | tf_op jit(solution)/shard_map/all_gather | solution.py:137
  8.7 3.9 copy-start.20
  14.2 138.8 %all-gather.6.cloned.1.call-start = ((), (), s32[]{:S(2)}) async-start(), calls=%async_computation.5 | async-start | bytes 4423680 | tf_op jit(solution)/shard_map/all_gather | solution.py:148
  112.7 4.9 copy-start.41
  112.7 4.9 copy-start.46
  117.6 3.1 copy-start.39
  122.0 87.5 %reduce-scatter.13.cloned.1.call-start = ((), (), s32[]{:S(2)}) async-start(), calls=%async_computation.9 | async-start | bytes 4423680
  168.9 45.1 %copy-start.42 = (f32[512]{0:T(512)S(1)}, f32[512]{0:T(512)}, u32[]{:S(2)}) copy-start(f32[512]{0:T(512)} %param.38) | copy-start | bytes 6148
  169.0 82.0 %all-gather.8.cloned.1.call-start = ((), (), s32[]{:S(2)}) async-start(), calls=%async_computation.6 | async-start | bytes 4423680 | tf_op jit(solution)/shard_map/all_gather | solution.py:177
  220.0 90.0 %reduce-scatter.15.cloned.1.call-start = ((), (), s32[]{:S(2)}) async-start(), calls=%async_computation.10 | async-start | bytes 4423680
  251.0 10.8 %copy-start.26 = (bf16[512,512]{1,0:T(8,128)(2,1)S(1)}, bf16[512,512]{1,0:T(8,128)(2,1)}, u32[]{:S(2)}) copy-start(bf16[512,512]{1,0:T(8,128)(2,1)} %param.35) | copy-start | bytes 1572868
  269.4 265.9 %all-reduce.6.cloned.1.call-start = ((), (), s32[]{:S(2)}) async-start(), calls=%async_computation.11 | async-start | bytes 14155776
  313.2 4.2 copy-start.4
  329.1 3.6 copy-start.16
  343.6 3.6 copy-start.16
  358.0 3.6 copy-start.16
  372.5 3.6 copy-start.16
  402.9 6.5 copy-start.47
  402.9 200.2 %reduce-scatter.9.cloned.1.call-start = ((), (), s32[]{:S(2)}) async-start(), calls=%async_computation.7 | async-start | bytes 1179648 | tf_op jit(solution)/shard_map/reduce_scatter | solution.py:203
  409.3 260.7 %reduce-scatter.11.cloned.1.call-start = ((), (), s32[]{:S(2)}) async-start(), calls=%async_computation.8 | async-start | bytes 1179648 | tf_op jit(solution)/shard_map/reduce_scatter | solution.py:204
  410.6 8.4 %copy-start.8 = (bf16[4,216,8,64]{1,3,2,0:T(8,128)(2,1)S(1)}, bf16[4,216,8,64]{1,3,2,0:T(8,128)(2,1)}, u32[]{:S(2)}) copy-start(bf16[4,216,8,64]{1,3,2,0:T(8,128)(2,1)} %get-tuple-element.103) | copy-start | bytes 2654212
  419.0 402.9 %all-reduce.8.cloned.1.call-start = ((), (), s32[]{:S(2)}) async-start(), calls=%async_computation.12 | async-start | bytes 8781824 | tf_op jit(solution)/shard_map/psum | solution.py:253
  421.7 6.5 copy-start.3
  421.7 6.5 copy-start.19
  429.9 108.4 %copy-start.31 = (bf16[512,512]{1,0:T(8,128)(2,1)S(1)}, bf16[512,512]{1,0:T(8,128)(2,1)}, u32[]{:S(2)}) copy-start(bf16[512,512]{1,0:T(8,128)(2,1)} %param.28) | copy-start | bytes 1572868
  821.9 6.4 copy-start.23
  821.9 7.3 copy-start.22
  823.7 6.5 copy-start.1
  (44 other events, 88.6 us)
Sparse Core Ops, SparseCore 0:
  14.3 53.5 all-gather.3
  122.2 30.7 all-gather.5
  169.1 40.4 reduce-scatter.12
  220.2 30.7 all-gather.7
  269.6 40.4 reduce-scatter.14
  403.0 132.3 all-reduce.5
  539.4 63.6 reduce-scatter.8
  607.4 62.4 reduce-scatter.10
  677.6 144.2 all-reduce.7
where the time goes:
time: 847 us; the launch traced here: 837 us
  waiting for transfers between devices  526 us (62%)
  matrix products  120 us (14%)
  local copies, waits for them, and re-layouts  98.7 us (12%)
  blocking collectives  40.5 us (5%)
  other arithmetic  33.6 us (4%)
  between operations  15.5 us (2%)
    unnamed x12, waiting for transfers between devices  184 us
    psum x1, waiting for transfers between devices, body(): lax.psum((embed_weight_grad, embed_bias_grad, query_weight_grad, query_bi...  152 us
    reduce_scatter x1, waiting for transfers between devices, body(): lax.psum_scatter(down_share, 'dp', scatter_dimension=1, tiled=True)  66.9 us
    all_gather x1, waiting for transfers between devices, body(): key_value_all = lax.all_gather(key_value, 'tensor', axis=1, tiled=True)  48.5 us
    psum x1, blocking collectives, body(): lax.psum((embed_weight_grad, embed_bias_grad, query_weight_grad, query_bi...  40.5 us
    unnamed x104, local copies, waits for them, and re-layouts  39.9 us
    all_gather x1, waiting for transfers between devices, body(): lax.all_gather(first_low.reshape(windows, own_rows, model_width), 'tensor...  30.7 us
    all_gather x1, waiting for transfers between devices, body(): lax.all_gather(grad_branch.reshape(windows, own_rows, model_width), 'tens...  30.5 us
  transfers between devices with their start and end apart: 9, of which 9 were waited for; matrix products, arithmetic and copies ran while one was open for 5% of the time, Pallas kernels for 0%

commit v1 on v0

v1 whole, which is shorter than its diff:
```python
import functools
import jax
import jax.numpy as jnp
from jax import lax
from jax.experimental import pallas as pl
from jax.experimental.pallas import tpu as pltpu
from jax.sharding import PartitionSpec as P

HEADS = 8
EPSILON = 1e-05
F32 = jnp.float32
BF16 = jnp.bfloat16
MESH = pl.DeviceIdType.MESH
GELU_A = 0.7978845608028654
GELU_B = GELU_A * 0.044715
MASKED = -1e30

EMBED, QUERY, VALUE, OUT, GAIN1, SHIFT1, DOWN, GAIN2, SHIFT2, UP = range(10)


def mm(left, right, cl=1, cr=0):
    return lax.dot_general(
        left, right, (((cl,), (cr,)), ((), ())), preferred_element_type=F32
    )


def row_mean(x):
    return jnp.mean(x, axis=1, keepdims=True)


def col_sum(x):
    return jnp.sum(x, axis=0, keepdims=True)


def pad_rows(x, rows):
    if x.shape[0] == rows:
        return x
    return jnp.concatenate([x, jnp.zeros((rows - x.shape[0], x.shape[1]), x.dtype)], axis=0)


class Sems:
    def __init__(self, send, recv):
        self.send, self.recv, self.used = send, recv, 0

    def copy(self, src, dst, device):
        i = self.used
        self.used += 1
        return pltpu.make_async_remote_copy(
            src_ref=src,
            dst_ref=dst,
            send_sem=self.send.at[i],
            recv_sem=self.recv.at[i],
            device_id=device,
            device_id_type=MESH,
        )

    def local(self, src, dst):
        i = self.used
        self.used += 1
        return pltpu.make_async_copy(src, dst, self.send.at[i])

    def slot(self):
        i = self.used
        self.used += 1
        return self.send.at[i], self.recv.at[i]


N_SEMS = 160
DIRECT = 4


def doublings(nz):
    assert nz & (nz - 1) == 0
    return nz.bit_length() - 1


def kernel(
    cfg,
    series, cot_in, w_embed, w_q, w_k, w_v, w_o, w_up, w_down, vec, ub_in,
    o_mixed, o_series, o_qkv, o_out, o_up, o_down, o_tail,
    xs, xp, en, elow, qkv, prob, ds, mxf, mx, rinv, inv1, flow, hid, slope, cot, g2, gb,
    qt, dt, wb, wqkv, wo, we, ubb,
    g, rc, r1, r2, rz,
    gq, rcq, r1q, r2q, rzq,
    go, rco, r1o, r2o, rzo,
    tb, rt, rtz,
    bv, send, recv,
):
    blocks, rows, padded, nz, fr = cfg
    n = blocks * padded
    width = wo.shape[0]
    pairs = qkv.shape[0]
    dp, t = lax.axis_index("dp"), lax.axis_index("tensor")
    c, y = t % 2, t // 2
    b, z = dp % 2, dp // 2
    co, yo, bo = 1 - c, 1 - y, 1 - b
    sems = Sems(send, recv)

    def dev(cc, yy, bb, zz=None):
        return ((z if zz is None else zz) * 2 + bb, yy * 2 + cc)

    core_dev, y_dev, x_dev = dev(co, y, b), dev(c, yo, b), dev(c, y, bo)
    peers = []
    for k in range(1, 8):
        peers.append((
            co if k & 4 else c,
            yo if k & 2 else y,
            bo if k & 1 else b,
        ))

    barrier = pltpu.get_barrier_semaphore()
    for pc, py, pb in peers:
        pl.semaphore_signal(barrier, inc=1, device_id=dev(pc, py, pb), device_id_type=MESH)
    for k in range(1, nz):
        pl.semaphore_signal(
            barrier, inc=1, device_id=dev(c, y, b, (z + k) % nz), device_id_type=MESH
        )

    load_we = sems.local(w_embed, we)
    load_we.start()
    own_x = sems.local(series.at[t], xs.at[t])
    own_x.start()
    load_qkv = []
    for p in range(pairs):
        for j, w in enumerate((w_q, w_k, w_v)):
            cp = sems.local(
                w.at[:, 128 * p:128 * p + 128], wqkv.at[p, :, 128 * j:128 * j + 128]
            )
            cp.start()
            load_qkv.append(cp)
    load_wo = sems.local(w_o, wo)
    load_wo.start()
    own_w = [sems.local(w, wb.at[m, t]) for m, w in enumerate((w_up, w_down))]
    for cp in own_w:
        cp.start()
    own_cot = sems.local(cot_in.at[t], cot.at[t])
    own_cot.start()
    ubb[t] = ub_in[...]
    bv[...] = jnp.zeros_like(bv)

    pl.semaphore_wait(barrier, 7 + nz - 1)

    def exchange(src, dst):
        out = []
        for k in range(1, blocks):
            other = (t + k) % blocks
            out.append(sems.copy(src.at[other], dst.at[t], (dp, other)))
        return out

    send_x = exchange(series, xs)
    for cp in send_x:
        cp.start()

    hidden = w_up.shape[0]
    part = hidden // 4
    t_y = yo * 2 + c
    stage_y = []
    for m, w in enumerate((w_up, w_down)):
        for s in range(2):
            at = pl.ds(pl.multiple_of(b * 2 * part + s * part, part), part)
            stage_y.append((m, at, sems.copy(w.at[at], wb.at[m, t, at], y_dev)))
    for _, _, cp in stage_y:
        cp.start()
    stage_core = [
        sems.copy(w, wb.at[m, t], core_dev) for m, w in enumerate((w_up, w_down))
    ]
    for cp in stage_core:
        cp.start()
    stage_ub = []
    for k in range(1, blocks):
        other = (t + k) % blocks
        stage_ub.append(sems.copy(ub_in, ubb.at[t], (dp, other)))
    for cp in stage_ub:
        cp.start()

    stage_x, stage_d, stage_e = [], [], []

    def weights_forward_y():
        for m, at, cp in stage_y:
            cp.wait_recv()
            nxt = sems.copy(wb.at[m, t_y, at], wb.at[m, t_y, at], x_dev)
            nxt.start()
            stage_x.append((m, nxt))
            fwd = sems.copy(wb.at[m, t_y, at], wb.at[m, t_y, at], core_dev)
            fwd.start()
            stage_d.append(fwd)

    def weights_forward_x():
        for i, (m, cp) in enumerate(stage_x):
            cp.wait_recv()
            s = i % 2
            at = pl.ds(pl.multiple_of(bo * 2 * part + s * part, part), part)
            fwd = sems.copy(wb.at[m, t_y, at], wb.at[m, t_y, at], core_dev)
            fwd.start()
            stage_e.append(fwd)

    def weights_ready():
        for cp in own_w:
            cp.wait()
        for cp in stage_core + stage_ub + stage_d + stage_e:
            cp.wait_recv()
        for cp in stage_core + stage_ub + stage_d + stage_e:
            cp.wait_send()
        for _, _, cp in stage_y:
            cp.wait_send()
        for _, cp in stage_x:
            cp.wait_send()

    load_we.wait()
    own_x.wait()
    for cp in send_x:
        cp.wait()
    for i in range(blocks):
        x = xs[i]
        e = mm(x, we[...]) + vec[EMBED:EMBED + 1, :]
        at = pl.ds(i * padded, padded)
        e = pad_rows(e, padded)
        en[at, :] = e
        elow[at, :] = e.astype(BF16)
        xp[at, :] = pad_rows(x.astype(F32), padded).astype(BF16)
    for cp in load_qkv:
        cp.wait()

    def project(p, carry):
        lanes = pl.ds(pl.multiple_of(p * 128, 128), 128)
        out = mm(elow[...], wqkv[p])
        q = (out[:, :128] + vec[QUERY:QUERY + 1, lanes]).astype(BF16)
        qkv[p, :, 0:128] = q * jnp.asarray(0.125, BF16)
        qkv[p, :, 128:256] = out[:, 128:256].astype(BF16)
        qkv[p, :, 256:384] = (out[:, 256:384] + vec[VALUE:VALUE + 1, lanes]).astype(BF16)
        qkv[p, :, 384:512] = jnp.ones((n, 128), BF16)
        return carry

    lax.fori_loop(0, pairs, project, 0)

    weights_forward_y()
    send_cot = exchange(cot_in, cot)
    for cp in send_cot:
        cp.start()

    lane = lax.broadcasted_iota(jnp.int32, (1, 128), 1)
    key_at = lax.broadcasted_iota(jnp.int32, (1, n), 1)
    mask = jnp.where(key_at % padded >= rows, MASKED, 0.0).astype(F32)

    tile_f = 128

    def attend_pair(p):
        def attend_tile(i, carry):
            at = pl.ds(pl.multiple_of(i * tile_f, tile_f), tile_f)
            q = qkv[p, at, 0:128]
            outs, inverses = [], []
            for h in range(2):
                qm = jnp.where((lane // 64) == h, q, jnp.zeros_like(q))
                s = mm(qm, qkv[p, :, 128:256], 1, 1) + mask
                e = jnp.exp(s - jnp.max(s, axis=1, keepdims=True)).astype(BF16)
                prob[2 * p + h, at, :] = e
                o = mm(e, qkv[p, :, 256:512])
                outs.append(o[:, :128])
                inverses.append(1.0 / o[:, 128:])
            inverse = jnp.where(lane < 64, inverses[0], inverses[1])
            o = jnp.where(lane < 64, outs[0], outs[1]) * inverse
            lanes = pl.ds(pl.multiple_of(p * 128, 128), 128)
            mxf[at, lanes] = o
            mx[at, lanes] = o.astype(BF16)
            rinv[at, lanes] = inverse.astype(BF16)
            return carry

        lax.fori_loop(0, n // tile_f, attend_tile, 0, unroll=True)

    def attend_some(p, carry):
        attend_pair(p)
        return carry

    lax.fori_loop(0, pairs - 1, attend_some, 0)
    weights_forward_x()
    lax.fori_loop(pairs - 1, pairs, attend_some, 0)

    load_wo.wait()

    def first_norm(i, carry):
        at = pl.ds(pl.multiple_of(i * padded, padded), padded)
        zz = en[at, :] + (mm(mx[at, :], wo[...]) + vec[OUT:OUT + 1, :])
        centred = zz - row_mean(zz)
        inv = lax.rsqrt(row_mean(centred * centred) + EPSILON)
        nn = centred * inv
        en[at, :] = nn
        inv1[at, :] = jnp.broadcast_to(inv, (padded, 128))
        flow[at, :] = (nn * vec[GAIN1:GAIN1 + 1, :] + vec[SHIFT1:SHIFT1 + 1, :]).astype(BF16)
        return carry

    lax.fori_loop(0, blocks, first_norm, 0)
    weights_ready()
    own_cot.wait()
    for cp in send_cot:
        cp.wait()

    def feed_forward(i, carry):
        at = pl.ds(pl.multiple_of(i * padded, padded), padded)
        fl = flow[at, :]
        acc = en[at, :] * vec[GAIN1:GAIN1 + 1, :] + vec[SHIFT1:SHIFT1 + 1, :]
        acc = acc + vec[DOWN:DOWN + 1, :]
        for j in range(blocks):
            v = mm(fl, wb[0, j], 1, 1) + ubb[j, 0:1, :]
            v2 = v * v
            half = 0.5 * jnp.tanh(v * (GELU_A + GELU_B * v2)) + 0.5
            h = v * half
            slope[j, at, :] = (
                half + h * (1.0 - half) * (2 * GELU_A + (6 * GELU_B) * v2)
            ).astype(BF16)
            h = h.astype(BF16)
            hid[j, at, :] = h
            acc = acc + mm(h, wb[1, j])
        centred = acc - row_mean(acc)
        inv = lax.rsqrt(row_mean(centred * centred) + EPSILON)
        nn = centred * inv
        up = pad_rows(cot[i].astype(F32), padded)
        result = nn * vec[GAIN2:GAIN2 + 1, :] + vec[SHIFT2:SHIFT2 + 1, :]
        cot[i] = result[:rows].astype(BF16)
        gg = up * vec[GAIN2:GAIN2 + 1, :]
        back = inv * (gg - row_mean(gg) - nn * row_mean(gg * nn))
        g2[at, :] = back
        low = back.astype(BF16)
        gb[at, :] = low
        bv[GAIN2:GAIN2 + 1, :] += col_sum(up * nn)
        bv[SHIFT2:SHIFT2 + 1, :] += col_sum(up)
        bv[DOWN:DOWN + 1, :] += col_sum(low.astype(F32))
        return carry

    lax.fori_loop(0, blocks, feed_forward, 0)

    own_mixed = sems.local(cot.at[t], o_mixed.at[t])
    own_mixed.start()
    send_mixed = exchange(cot, o_mixed)
    for cp in send_mixed:
        cp.start()

    def add_into(dst, src, index):
        dst[index] = (dst[index].astype(F32) + src[...].astype(F32)).astype(BF16)

    class FeedSum:
        def __init__(self, m, out):
            self.m, self.out = m, out

        def core(self):
            m = self.m
            self.cps = []
            for yy in range(2):
                cp = sems.copy(g.at[m, yy * 2 + co], rc.at[m, yy], core_dev)
                cp.start()
                self.cps.append(cp)

        def first(self):
            m = self.m
            for yy, cp in enumerate(self.cps):
                cp.wait()
                for bb in range(2):
                    for zz in range(nz):
                        add_into(g, rc.at[m, yy, bb, zz], (m, yy * 2 + c, bb, zz))
            self.cps = []
            if m == 1:
                cp = sems.copy(g.at[m, yo * 2 + c], r1.at[m], y_dev)
                cp.start()
                self.cps.append(cp)
            else:
                for yy in range(2):
                    cp = sems.copy(g.at[m, yy * 2 + c, bo], r1.at[m, yy], x_dev)
                    cp.start()
                    self.cps.append(cp)

        def second(self):
            m = self.m
            for cp in self.cps:
                cp.wait()
            if m == 1:
                for bb in range(2):
                    for zz in range(nz):
                        add_into(g, r1.at[m, bb, zz], (m, t, bb, zz))
                cp = sems.copy(g.at[m, t, bo], r2.at[m], x_dev)
            else:
                for yy in range(2):
                    for zz in range(nz):
                        add_into(g, r1.at[m, yy, zz], (m, yy * 2 + c, b, zz))
                cp = sems.copy(g.at[m, yo * 2 + c, b], r2.at[m], y_dev)
            cp.start()
            self.cps = [cp]

        def third(self):
            m = self.m
            for cp in self.cps:
                cp.wait()
            for zz in range(nz):
                add_into(g, r2.at[m, zz], (m, t, b, zz))
            self.cps = []
            for k in range(1, nz):
                zz = (z + k) % nz
                cp = sems.copy(g.at[m, t, b, zz], rz.at[m, k - 1], dev(c, y, b, zz))
                cp.start()
                self.cps.append(cp)

        def last(self):
            m = self.m
            for cp in self.cps:
                cp.wait()
            total = g[m, t, b, z].astype(F32)
            for k in range(nz - 1):
                total = total + rz[m, k].astype(F32)
            self.out[...] = total

    class MatrixSum:
        def __init__(self, grad, rcv, rcv1, rcv2, rcvz, out, y_first):
            self.refs = (grad, rcv, rcv1, rcv2, rcvz, out)
            self.y_first = y_first

        def start(self, src, dst, device):
            cp = sems.copy(src, dst, device)
            cp.start()
            self.cps.append(cp)

        def wait(self):
            for cp in self.cps:
                cp.wait()
            self.cps = []

        def steps(self):
            grad, rcv, rcv1, rcv2, rcvz, out = self.refs
            self.cps = []
            self.start(grad.at[co], rcv, core_dev)
            yield
            self.wait()
            for yy in range(2):
                for bb in range(2):
                    add_into(grad, rcv.at[yy, bb], (c, yy, bb))
            if self.y_first:
                self.start(grad.at[c, yo], rcv1, y_dev)
            else:
                for yy in range(2):
                    self.start(grad.at[c, yy, bo], rcv1.at[yy], x_dev)
            yield
            self.wait()
            for i in range(2):
                add_into(grad, rcv1.at[i], (c, y, i) if self.y_first else (c, i, b))
            if self.y_first:
                self.start(grad.at[c, y, bo], rcv2, x_dev)
            else:
                self.start(grad.at[c, yo, b], rcv2, y_dev)
            yield
            self.wait()
            add_into(grad, rcv2, (c, y, b))
            if nz <= DIRECT:
                rcvz[z] = grad[c, y, b]
                for k in range(1, nz):
                    self.start(grad.at[c, y, b], rcvz.at[z], dev(c, y, b, (z + k) % nz))
                yield
                self.wait()
                total = rcvz[0].astype(F32)
                for k in range(1, nz):
                    total = total + rcvz[k].astype(F32)
                out[c, y, b] = total.astype(BF16)
            else:
                for s in range(doublings(nz)):
                    far = z + 2**s * (1 - 2 * ((z // 2**s) % 2))
                    self.start(grad.at[c, y, b], rcvz.at[s], dev(c, y, b, far))
                    yield
                    self.wait()
                    add_into(grad, rcvz.at[s], (c, y, b))
                out[c, y, b] = grad[c, y, b]
            if self.y_first:
                self.start(out.at[c, y, b], out.at[c, y, b], x_dev)
            else:
                self.start(out.at[c, y, b], out.at[c, y, b], y_dev)
            yield
            self.wait()
            if self.y_first:
                self.start(out.at[c, y], out.at[c, y], y_dev)
            else:
                for yy in range(2):
                    self.start(out.at[c, yy, b], out.at[c, yy, b], x_dev)
            yield
            self.wait()
            self.start(out.at[c], out.at[c], core_dev)
            yield
            self.wait()

    down_sum, up_sum = FeedSum(0, o_down), FeedSum(1, o_up)

    def feed_grad(m, left, right):
        def one(j, carry):
            out = mm(left, right[j], 0, 0).astype(BF16)
            for zz in range(nz):
                for bb in range(2):
                    i = (zz * 2 + bb) * fr
                    g[m, j, bb, zz] = out[i:i + fr]
            return carry

        lax.fori_loop(0, blocks, one, 0)

    feed_grad(0, gb[...], hid)
    down_sum.core()

    load_out = []

    def feed_back(i, carry):
        at = pl.ds(pl.multiple_of(i * padded, padded), padded)
        low = gb[at, :]
        acc = g2[at, :]
        for j in range(blocks):
            gp = (slope[j, at, :].astype(F32) * mm(low, wb[1, j], 1, 1)).astype(BF16)
            slope[j, at, :] = gp
            bv[UP + j:UP + j + 1, :] += col_sum(gp.astype(F32))
            acc = acc + mm(gp, wb[0, j])
        nn = en[at, :]
        bv[GAIN1:GAIN1 + 1, :] += col_sum(acc * nn)
        bv[SHIFT1:SHIFT1 + 1, :] += col_sum(acc)
        gg = acc * vec[GAIN1:GAIN1 + 1, :]
        inv = inv1[at, 0:1]
        back = inv * (gg - row_mean(gg) - nn * row_mean(gg * nn))
        g2[at, :] = back
        ga = back.astype(BF16)
        flow2 = ga
        bv[OUT:OUT + 1, :] += col_sum(ga.astype(F32))
        gm = mm(ga, wo[...], 1, 1)
        gb[at, :] = (gm * rinv[at, :].astype(F32)).astype(BF16)
        hid[0, at, :] = flow2
        return carry

    lax.fori_loop(0, blocks, feed_back, 0)
    down_sum.first()
    feed_grad(1, flow[...], slope)
    up_sum.core()

    out_sum = MatrixSum(go, rco, r1o, r2o, rzo, o_out, True)
    out_grad = mm(mx[...], hid[0], 0, 0).astype(BF16)
    for i in range(8):
        r = width // 8
        go[i // 4, (i // 2) % 2, i % 2] = out_grad[i * r:(i + 1) * r]
    out_steps = out_sum.steps()
    next(out_steps)

    tile_b = n // 2
    zs = rzo.shape[0]
    pair_sums = []

    def attend_back(p):
        lanes = pl.ds(p * 128, 128)
        qt[...] = qkv[p, :, 0:128].T
        dt[...] = gb[:, lanes].T
        for h in range(2):
            def tile(i, carry):
                at = pl.ds(pl.multiple_of(i * tile_b, tile_b), tile_b)
                d = gb[at, lanes]
                own = (lane // 64) == h
                dm = jnp.where(own, d, jnp.zeros_like(d))
                centre = jnp.sum(
                    jnp.where(own, d.astype(F32) * mxf[at, lanes], 0.0), axis=1, keepdims=True
                )
                s = (mm(dm, qkv[p, :, 256:384], 1, 1) - centre).astype(BF16)
                s = s * prob[2 * p + h, at, :]
                ds[at, :] = s
                dq = mm(s, qkv[p, :, 128:256])
                if h == 0:
                    mxf[at, lanes] = jnp.where(lane < 64, dq, mxf[at, lanes])
                else:
                    dq = jnp.where(lane < 64, mxf[at, lanes], dq) * 0.125
                    rinv[at, lanes] = dq.astype(BF16)
                return carry

            lax.fori_loop(0, n // tile_b, tile, 0, unroll=True)
            half = slice(64 * h, 64 * h + 64)
            dk = mm(qt[half, :], ds[...])
            dv = mm(dt[half, :], prob[2 * p + h])
            qt[half, :] = dk.astype(BF16)
            dt[half, :] = dv.astype(BF16)
        dq = rinv[:, lanes]
        dv = dt[...].T
        qkv[p, :, 0:128] = dq
        qkv[p, :, 128:256] = qt[...].T
        qkv[p, :, 256:384] = dv
        bv[QUERY:QUERY + 1, lanes] += col_sum(dq.astype(F32))
        bv[VALUE:VALUE + 1, lanes] += col_sum(dv.astype(F32))
        grads = qkv[p, :, 0:384]
        grad = mm(elow[...], grads, 0, 0).astype(BF16)
        for i in range(8):
            r = width // 8
            gq[p, i // 4, (i // 2) % 2, i % 2] = grad[i * r:(i + 1) * r]
        one = MatrixSum(
            gq.at[p], rcq.at[p], r1q.at[p], r2q.at[p], rzq.at[p], o_qkv.at[p], p % 2 == 1
        )
        steps = one.steps()
        next(steps)
        pair_sums.append(steps)
        g2[...] += mm(grads, wqkv[p], 1, 1)

    def advance(steps):
        next(steps, None)

    attend_back(0)
    down_sum.second()
    up_sum.first()
    advance(out_steps)
    attend_back(1)
    down_sum.third()
    up_sum.second()
    advance(out_steps)
    advance(pair_sums[0])
    attend_back(2)
    down_sum.last()
    up_sum.third()
    advance(out_steps)
    advance(pair_sums[0])
    advance(pair_sums[1])
    attend_back(3)
    up_sum.last()
    advance(out_steps)
    for i in (0, 1, 2):
        advance(pair_sums[i])

    low = g2[...].astype(BF16)
    bv[EMBED:EMBED + 1, :] += col_sum(low.astype(F32))
    grad = mm(xp[...], low, 0, 0)
    look = grad.shape[0]
    whole = jnp.concatenate(
        [grad, bv[0:UP + blocks, :], jnp.zeros((128 - look - UP - blocks, width), F32)], axis=0
    ).astype(BF16)
    for i in range(8):
        tb[i] = whole[16 * i:16 * i + 16]
    me = c * 4 + y * 2 + b
    tail = []
    for k, (pc, py, pb) in enumerate(peers):
        cp = sems.copy(tb.at[pc * 4 + py * 2 + pb], rt.at[k], dev(pc, py, pb))
        cp.start()
        tail.append(cp)
    out = mm(low, we[...], 1, 1)
    for i in range(blocks):
        xs[i] = out[i * padded:i * padded + rows].astype(BF16)
    own_s = sems.local(xs.at[t], o_series.at[t])
    own_s.start()
    send_s = exchange(xs, o_series)
    for cp in send_s:
        cp.start()
    advance(out_steps)
    for i in (0, 1, 2, 3):
        advance(pair_sums[i])
    for cp in tail:
        cp.wait()
    total = tb[me].astype(F32)
    for k in range(7):
        total = total + rt[k].astype(F32)
    tb[me] = total.astype(BF16)
    tail = []
    rtz[z] = tb[me]
    for k in range(1, nz):
        cp = sems.copy(tb.at[me], rtz.at[z], dev(c, y, b, (z + k) % nz))
        cp.start()
        tail.append(cp)
    for i in (0, 1, 2, 3):
        advance(pair_sums[i])
    advance(out_steps)
    for cp in tail:
        cp.wait()
    total = rtz[0].astype(F32)
    for k in range(1, nz):
        total = total + rtz[k].astype(F32)
    o_tail[me] = total.astype(BF16)
    tail = []
    for pc, py, pb in peers:
        cp = sems.copy(o_tail.at[me], o_tail.at[me], dev(pc, py, pb))
        cp.start()
        tail.append(cp)
    for _ in range(8 + zs):
        advance(out_steps)
        for i in (0, 1, 2, 3):
            advance(pair_sums[i])
    for cp in tail + send_s + send_mixed:
        cp.wait()
    own_s.wait()
    own_mixed.wait()


def body(
    series, embed_weight, embed_bias, query_weight, query_bias, key_weight, value_weight,
    value_bias, out_weight, out_bias, first_gain, first_shift, up_weight, up_bias,
    down_weight, down_bias, second_gain, second_shift, cotangent,
    *, dp_size, tensor_size,
):
    windows, rows, look = series.shape
    width = embed_weight.shape[1]
    hidden = up_weight.shape[0]
    pairs = HEADS // 2
    assert windows == tensor_size == 4 and width == HEADS * 64 and dp_size % 2 == 0
    padded = -(-rows // 32) * 32
    n = tensor_size * padded
    nz = dp_size // 2
    fr = width // dp_size
    r = width // 8
    zs = nz if nz <= DIRECT else doublings(nz)

    vec = jnp.stack([
        embed_bias, query_bias, value_bias, out_bias, first_gain, first_shift, down_bias,
        second_gain, second_shift,
    ])
    vec = jnp.pad(vec, ((0, 16 - vec.shape[0]), (0, 0)))
    ub = jnp.broadcast_to(up_bias.astype(F32)[None, :], (8, hidden))

    def scr(*shape, dtype=BF16):
        return pltpu.VMEM(shape, dtype)

    scratch = [
        scr(4, rows, look),
        scr(n, look),
        scr(n, width, dtype=F32),
        scr(n, width),
        scr(pairs, n, 512),
        scr(HEADS, n, n),
        scr(n, n),
        scr(n, width, dtype=F32),
        scr(n, width),
        scr(n, width),
        scr(n, 128, dtype=F32),
        scr(n, width),
        scr(4, n, hidden),
        scr(4, n, hidden),
        scr(4, rows, width),
        scr(n, width, dtype=F32),
        scr(n, width),
        scr(128, n),
        scr(128, n),
        scr(2, 4, hidden, width),
        scr(pairs, width, 384),
        scr(width, width),
        scr(look, width),
        scr(4, 8, hidden, dtype=F32),
        scr(2, 4, 2, nz, fr, hidden),
        scr(2, 2, 2, nz, fr, hidden),
        scr(2, 2, nz, fr, hidden),
        scr(2, nz, fr, hidden),
        scr(2, nz - 1, fr, hidden),
        scr(pairs, 2, 2, 2, r, 384),
        scr(pairs, 2, 2, r, 384),
        scr(pairs, 2, r, 384),
        scr(pairs, r, 384),
        scr(pairs, zs, r, 384),
        scr(2, 2, 2, r, width),
        scr(2, 2, r, width),
        scr(2, r, width),
        scr(r, width),
        scr(zs, r, width),
        scr(8, 16, width),
        scr(7, 16, width),
        scr(nz, 16, width),
        scr(16, width, dtype=F32),
        pltpu.SemaphoreType.DMA((N_SEMS + 16 * nz,)),
        pltpu.SemaphoreType.DMA((N_SEMS + 16 * nz,)),
    ]
    hbm = pl.BlockSpec(memory_space=pl.ANY)
    vmem = pl.BlockSpec(memory_space=pltpu.VMEM)
    sd = jax.ShapeDtypeStruct
    mixed, sgrad, g_qkv, g_out, g_up, g_down, tail = pl.pallas_call(
        functools.partial(kernel, (4, rows, padded, nz, fr)),
        out_shape=[
            sd((4, rows, width), BF16),
            sd((4, rows, look), BF16),
            sd((pairs, 2, 2, 2, r, 384), BF16),
            sd((2, 2, 2, r, width), BF16),
            sd((fr, hidden), F32),
            sd((fr, hidden), F32),
            sd((8, 16, width), BF16),
        ],
        in_specs=[hbm] * 9 + [vmem] * 2,
        out_specs=[hbm] * 2 + [vmem] * 5,
        scratch_shapes=scratch,
        compiler_params=pltpu.CompilerParams(
            collective_id=1, has_side_effects=True, vmem_limit_bytes=64 * 1024 * 1024
        ),
    )(
        series, cotangent, embed_weight, query_weight, key_weight, value_weight, out_weight,
        up_weight, down_weight, vec, ub,
    )
    g_qkv = g_qkv.reshape(pairs, width, 3, 128).astype(F32)
    g_qkv = g_qkv.transpose(2, 1, 0, 3).reshape(3, width, width)
    tail = tail.reshape(128, width).astype(F32)
    vecs = tail[look:look + UP + 4]
    return (
        mixed,
        sgrad,
        tail[:look],
        vecs[EMBED],
        g_qkv[0],
        vecs[QUERY],
        g_qkv[1],
        g_qkv[2],
        vecs[VALUE],
        g_out.reshape(width, width).astype(F32),
        vecs[OUT],
        vecs[GAIN1],
        vecs[SHIFT1],
        g_up.T,
        vecs[UP:UP + 4].reshape(4 * hidden),
        g_down.T,
        vecs[DOWN],
        vecs[GAIN2],
        vecs[SHIFT2],
    )


def solution(mesh):
    token = P("dp", "tensor", None)
    return jax.shard_map(
        functools.partial(
            body, dp_size=mesh.shape["dp"], tensor_size=mesh.shape["tensor"]
        ),
        mesh=mesh,
        in_specs=(
            token, P(), P(), P(), P(), P(), P(), P(), P(), P(), P(), P(),
            P("tensor", None), P("tensor"), P("tensor", None), P(), P(), P(), token,
        ),
        out_specs=(
            token, token, P(), P(), P(), P(), P(), P(), P(), P(), P(), P(), P(),
            P("tensor", "dp"), P(), P("tensor", "dp"), P(), P(), P(),
        ),
        check_vma=False,
    )
```

time: 847 us -> 179 us (0.21); the launches traced: 837 us -> 178 us
  waiting for transfers between devices: 526 us -> 0 us
  Pallas kernels: 0 us -> 143 us
  matrix products: 120 us -> 0 us
  local copies, waits for them, and re-layouts: 98.7 us -> 31.7 us
  blocking collectives: 40.5 us -> 0 us
  other arithmetic: 33.6 us -> 3.07 us
  between operations: 15.5 us -> 0.72 us
    unnamed x12 -> x0, waiting for transfers between devices: 184 us -> none
    psum x1 -> x0, waiting for transfers between devices: 152 us -> none  [body(): lax.psum((embed_weight_grad, embed_bias_grad, query_weight_grad, query_bi...]
    pallas_call x0 -> x1, Pallas kernels: none -> 143 us  [body(): pl.pallas_call(functools.partial(kernel, (4, rows, padded, nz, fr)), out_...]
    dot_general x49 -> x0, matrix products: 120 us -> none  [the longest x4 14.2 us: attend_back(): jnp.einsum('qhe,khe->hqk', grad_mixed, values_all, preferred_element_type...]
    all_gather x3 -> x0, waiting for transfers between devices: 110 us -> none  [the longest x1 48.5 us: body(): key_value_all = lax.all_gather(key_value, 'tensor', axis=1, tiled=True)]
    reduce_scatter x2 -> x0, waiting for transfers between devices: 81.4 us -> none  [the longest x1 66.9 us: body(): lax.psum_scatter(down_share, 'dp', scatter_dimension=1, tiled=True)]
    psum x1 -> x0, blocking collectives: 40.5 us -> none  [body(): lax.psum((embed_weight_grad, embed_bias_grad, query_weight_grad, query_bi...]
    unnamed x104 -> x20, local copies, waits for them, and re-layouts: 39.9 us -> 9.34 us
  transfers between devices with their start and end apart: 9 -> 0, of which waited for: 9 -> 0; matrix products, arithmetic and copies ran while one was open for 5% -> 0% of each run, Pallas kernels for 0% -> 0%
where the time goes in v1:
time: 179 us; the launch traced here: 178 us
  Pallas kernels  143 us (80%)
  local copies, waits for them, and re-layouts  31.7 us (18%)
  other arithmetic  3.07 us (2%)
    pallas_call x1, Pallas kernels, body(): pl.pallas_call(functools.partial(kernel, (4, rows, padded, nz, fr)), out_...  143 us
    unnamed x20, local copies, waits for them, and re-layouts  9.34 us
    slice x2, local copies, waits for them, and re-layouts, body(): g_qkv[2]  9.18 us
    transpose x1, local copies, waits for them, and re-layouts, body(): g_qkv = g_qkv.transpose(2, 1, 0, 3).reshape(3, width, width)  5.44 us

profile of v1, /device:TPU:0, one launch (start us, length us, event | category | flops | bytes accessed | tf_op | source)
XLA Modules:
  0.0 178.4 jit_solution(11460282696355904652)
XLA Ops:
  0.7 1.8 copy.45.series
  2.4 1.5 stack.39
  3.9 0.6 pad.4.vec
  4.5 1.3 broadcast_in_dim.2.ub_in
  5.8 142.9 %shard_map.330 = (bf16[4,216,512]{2,1,0:T(8,128)(2,1)}, bf16[4,216,96]{2,1,0:T(8,128)(2,1)}, bf16[4,2,2,2,64,384]{5,4,3,2,1,0:T(8,128)(2,1)}, bf16[2,2,2,64,512]...) custom-call(bf16[4,216,96]{2,1,0:T(8,128)(2,1)} %copy.45.series, ...), custom_call_target="tpu_custom_call" | custom-call | tf_op jit(solution)/shard_map/pallas_call | solution.py:757
  148.7 0.9 convert_element_type.22
  149.7 0.6 fusion.1
  150.3 5.4 %reshape.60 = f32[4,512,3,128]{3,2,1,0:T(4,128)} reshape(bf16[4,2,2,2,64,384]{5,4,3,2,1,0:T(8,128)(2,1)} %get-tuple-element.29) | data formatting | bytes 4718592 | tf_op jit(solution)/shard_map/transpose | solution.py:779
  155.7 8.5 %fusion = (f32[1,512,4,128]{3,0,1,2:T(1,128)S(1)}, f32[1,512,4,128]{3,0,1,2:T(1,128)S(1)}, f32[1,512,4,128]{3,0,1,2:T(1,128)}) fusion(f32[3,512,4,128]{3,0,1,2:T(4,128)} %bitcast.34), kind=kLoop, calls=%fused_computation.2 | loop fusion | bytes 6291456 | tf_op jit(solution)/shard_map/slice | solution.py:790
  164.3 2.3 %copy.46 = f32[1,512,4,128]{1,3,2,0:T(8,128)S(1)} copy(f32[1,512,4,128]{3,0,1,2:T(1,128)} %get-tuple-element.92) | data formatting | bytes 2097152 | tf_op jit(solution)/shard_map/slice | solution.py:787
  166.6 1.3 copy.50
  167.9 0.0 copy-start.1
  167.9 0.7 copy.47
  168.6 1.3 copy.51
  169.9 0.0 copy-start
  169.9 0.0 copy-start.3
  169.9 0.7 copy.48
  170.5 0.0 copy-start.2
  170.6 0.0 copy-start.4
  170.6 1.3 copy.52
  171.9 0.6 copy.53
  172.5 0.0 copy-done.1
  172.5 0.7 slice.74
  173.2 2.1 %bitcast_convert_fusion = f32[512,512]{1,0:T(8,128)} fusion(bf16[2,2,2,64,512]{4,3,2,1,0:T(8,128)(2,1)} %get-tuple-element.30), kind=kLoop, calls=%fused_computation | loop fusion | flops 262144 | bytes 1572864 | tf_op jit(solution)/shard_map/convert_element_type | solution.py:792
  175.3 0.0 copy-done.2
  175.3 0.8 copy.49
  176.1 0.0 copy-done
  176.1 0.9 copy.57
  177.1 0.0 copy-done.4
  177.1 0.7 copy.58
  177.7 0.0 copy-done.3
  177.7 0.7 copy.59
  (1 shorter events, 0.0 us)
Async XLA Ops:
  167.9 4.6 %copy-start.1 = (bf16[8,16,512]{2,1,0:T(8,128)(2,1)S(1)}, bf16[8,16,512]{2,1,0:T(8,128)(2,1)}, u32[]{:S(2)}) copy-start(bf16[8,16,512]{2,1,0:T(8,128)(2,1)} %get-tuple-element.28) | copy-start | bytes 393220
  169.9 6.3 %copy-start = (bf16[4,216,512]{2,1,0:T(8,128)(2,1)S(1)}, bf16[4,216,512]{2,1,0:T(8,128)(2,1)}, u32[]{:S(2)}) copy-start(bf16[4,216,512]{2,1,0:T(8,128)(2,1)} %get-tuple-element.121) | copy-start | bytes 2654212
  169.9 7.8 %copy-start.3 = (f32[64,512]{1,0:T(8,128)S(1)}, f32[64,512]{1,0:T(8,128)}, u32[]{:S(2)}) copy-start(f32[64,512]{1,0:T(8,128)} %get-tuple-element.32) | copy-start | bytes 393220
  170.5 4.8 %copy-start.2 = (bf16[4,216,96]{2,1,0:T(8,128)(2,1)S(1)}, bf16[4,216,96]{2,1,0:T(8,128)(2,1)}, u32[]{:S(2)}) copy-start(bf16[4,216,96]{2,1,0:T(8,128)(2,1)} %get-tuple-element.72) | copy-start | bytes 497668
  170.6 6.5 %copy-start.4 = (f32[64,512]{1,0:T(8,128)S(1)}, f32[64,512]{1,0:T(8,128)}, u32[]{:S(2)}) copy-start(f32[64,512]{1,0:T(8,128)} %get-tuple-element.31) | copy-start | bytes 393220

commit v2 on v1

v2 whole, which is shorter than its diff:
```python
import functools
import jax
import jax.numpy as jnp
from jax import lax
from jax.experimental import pallas as pl
from jax.experimental.pallas import tpu as pltpu
from jax.sharding import PartitionSpec as P

HEADS = 8
EPSILON = 1e-05
F32 = jnp.float32
BF16 = jnp.bfloat16
MESH = pl.DeviceIdType.MESH
GELU_A = 0.7978845608028654
GELU_B = GELU_A * 0.044715
MASKED = -1e30

EMBED, QUERY, VALUE, OUT, GAIN1, SHIFT1, DOWN, GAIN2, SHIFT2 = range(9)
S_GAIN1, S_SHIFT1, S_DOWN, S_GAIN2, S_SHIFT2, S_UP = range(1, 7)


def mm(left, right, cl=1, cr=0):
    return lax.dot_general(
        left, right, (((cl,), (cr,)), ((), ())), preferred_element_type=F32
    )


def row_mean(x):
    return jnp.mean(x, axis=1, keepdims=True)


def col_sum(x):
    return jnp.sum(x, axis=0, keepdims=True)


def pad_rows(x, rows):
    if x.shape[0] == rows:
        return x
    return jnp.concatenate([x, jnp.zeros((rows - x.shape[0], x.shape[1]), x.dtype)], axis=0)


class Sems:
    def __init__(self, send, recv):
        self.send, self.recv, self.used = send, recv, 0

    def copy(self, src, dst, device):
        i = self.used
        self.used += 1
        return pltpu.make_async_remote_copy(
            src_ref=src,
            dst_ref=dst,
            send_sem=self.send.at[i],
            recv_sem=self.recv.at[i],
            device_id=device,
            device_id_type=MESH,
        )

    def local(self, src, dst):
        i = self.used
        self.used += 1
        return pltpu.make_async_copy(src, dst, self.send.at[i])

    def slot(self):
        i = self.used
        self.used += 1
        return self.send.at[i], self.recv.at[i]


N_SEMS = 192


def kernel(
    cfg,
    series, cot_in, w_embed, w_q, w_k, w_v, w_o, w_up, w_down,
    b_embed, b_query, b_value, b_out, gain1, shift1, b_down, gain2, shift2, b_up,
    o_mixed, o_series, o_pairs, o_out, o_small, o_up, o_down,
    xs, xa, en, qkv, prob, ds, mxf, mx, rinv, inv1, flow, hid, slope, cot, g2, gb,
    qt, dt, wb, wqkv, wo, we, w2, ubb,
    g, rc, r1y, r1x, r2, rz,
    gp_, gprc, gpr1, gprz,
    go, gorc, gor1, gorz,
    gs, gsrc, gsr1, gsrz,
    vec, ubl, send, recv,
):
    blocks, rows, padded, nz, fr = cfg
    n = blocks * padded
    look = we.shape[0]
    width = wo.shape[0]
    pairs = qkv.shape[0]
    hidden = w_up.shape[0]
    lanes2 = hidden // 2
    dp, t = lax.axis_index("dp"), lax.axis_index("tensor")
    c, y = t % 2, t // 2
    b, z = dp % 2, dp // 2
    co, yo, bo = 1 - c, 1 - y, 1 - b
    xy = y * 2 + b
    sems = Sems(send, recv)

    def dev(cc, yy, bb, zz=None):
        return ((z if zz is None else zz) * 2 + bb, yy * 2 + cc)

    core_dev, y_dev, x_dev = dev(co, y, b), dev(c, yo, b), dev(c, y, bo)
    xy_peers = [(y, bo), (yo, b), (yo, bo)]

    barrier = pltpu.get_barrier_semaphore()
    partners = [dev(co, y, b), dev(co, yo, b)]
    partners += [dev(c, py, pb) for py, pb in xy_peers]
    partners += [dev(c, y, b, (z + k) % nz) for k in range(1, nz)]
    for partner in partners:
        pl.semaphore_signal(barrier, inc=1, device_id=partner, device_id_type=MESH)

    def load(src, dst):
        cp = sems.local(src, dst)
        cp.start()
        return cp

    load_we = load(w_embed, we)
    load_qkv = []
    for p in range(pairs):
        for j, w in enumerate((w_q, w_k, w_v)):
            load_qkv.append(load(
                w.at[:, 128 * p:128 * p + 128], wqkv.at[p, :, 128 * j:128 * j + 128]
            ))
    own_x = load(series.at[t], xs.at[t, 0:look])
    own_w = [load(w, wb.at[m, t]) for m, w in enumerate((w_up, w_down))]
    load_wo = load(w_o, wo)
    own_cot = load(cot_in.at[t], cot.at[t])
    for i, ref in enumerate(
        (b_embed, b_query, b_value, b_out, gain1, shift1, b_down, gain2, shift2)
    ):
        vec[i:i + 1, :] = ref[...]
    ubl[...] = jnp.broadcast_to(b_up[...].astype(F32), ubl.shape)
    ubb[t] = ubl[...]
    tail_rows = xs.shape[1] - look
    first = lax.broadcasted_iota(jnp.int32, (tail_rows, rows), 0) == 0
    for i in range(blocks):
        xs[i, look:, :] = jnp.where(first, 1.0, 0.0).astype(BF16)

    pl.semaphore_wait(barrier, len(partners))

    def exchange(src, dst, dst_at):
        out = []
        for k in range(1, blocks):
            other = (t + k) % blocks
            out.append(sems.copy(src.at[other], dst_at(dst), (dp, other)))
        return out

    send_x = exchange(series, xs, lambda r: r.at[t, 0:look])
    part = hidden // 4
    t_y, t_c, t_d = yo * 2 + c, y * 2 + co, yo * 2 + co
    stage_y, stage_core, stage_ub, stage_x, stage_d, stage_e = [], [], [], [], [], []
    for s in range(2):
        at = pl.ds(pl.multiple_of((b * 2 + s) * part, part), part)
        far = pl.ds(pl.multiple_of((bo * 2 + s) * part, part), part)
        for m, w in enumerate((w_up, w_down)):
            stage_y.append(sems.copy(w.at[at], wb.at[m, t, at], y_dev))
            stage_x.append(sems.copy(wb.at[m, t_y, at], wb.at[m, t_y, at], x_dev))
            stage_d.append(sems.copy(wb.at[m, t_y, at], wb.at[m, t_y, at], core_dev))
            stage_e.append(sems.copy(wb.at[m, t_y, far], wb.at[m, t_y, far], core_dev))
    for m, w in enumerate((w_up, w_down)):
        stage_core.append(sems.copy(w, wb.at[m, t], core_dev))
    for k in range(1, blocks):
        other = (t + k) % blocks
        stage_ub.append(sems.copy(ubl, ubb.at[t], (dp, other)))
    send_cot = exchange(cot_in, cot, lambda r: r.at[t])
    for cp in send_x + stage_ub + stage_y + stage_core + send_cot:
        cp.start()

    def forward_y(i):
        stage_y[i].wait_recv()
        stage_x[i].start()
        stage_d[i].start()

    def forward_x(i):
        stage_x[i].wait_recv()
        stage_e[i].start()

    load_we.wait()
    one_row = lax.broadcasted_iota(jnp.int32, (128, 1), 0)
    b_high = vec[EMBED:EMBED + 1, :].astype(BF16)
    b_low = vec[EMBED:EMBED + 1, :] - b_high.astype(F32)
    we_rows = pad_rows(we[...].astype(F32), 128)
    high = we_rows + jnp.where(one_row == look, b_high.astype(F32), 0.0)
    low = jnp.where(one_row == look, b_low, 0.0)
    w2[0, 0:128, :] = high.astype(BF16)
    w2[0, 128:256, :] = low.astype(BF16)
    both = (high + jnp.where(one_row == look + 1, b_low, 0.0)).astype(BF16)
    for cp in load_qkv:
        cp.wait()
    for p in range(pairs):
        at = slice(128 * p, 128 * p + 128)
        prod = mm(both, wqkv[p])
        bias = prod[look:look + 1] + prod[look + 1:look + 2]
        bias = bias + jnp.concatenate(
            [vec[QUERY:QUERY + 1, at], jnp.zeros((1, 128), F32), vec[VALUE:VALUE + 1, at]],
            axis=1,
        )
        prod = jnp.where(one_row < look, prod, jnp.where(one_row == look, bias, 0.0))
        factor = lax.broadcasted_iota(jnp.int32, (1, 384), 1)
        prod = prod * jnp.where(factor < 128, 0.125, 1.0)
        high = prod.astype(BF16)
        w2[1 + p, 0:128, 0:384] = high
        w2[1 + p, 128:256, 0:384] = (prod - high.astype(F32)).astype(BF16)
        qkv[p, :, 384:512] = jnp.ones((n, 128), BF16)

    own_x.wait()
    for cp in send_x:
        cp.wait()
    for i in range(blocks):
        x = pad_rows(xs[i].astype(F32).T, padded).astype(BF16)
        at = pl.ds(i * padded, padded)
        xa[at, 0:128] = x
        xa[at, 128:256] = x
    en[...] = mm(xa[...], w2[0])

    def project(p, carry):
        qkv[p, :, 0:384] = mm(xa[...], w2[1 + p, :, 0:384]).astype(BF16)
        return carry

    lax.fori_loop(0, pairs, project, 0)

    lane = lax.broadcasted_iota(jnp.int32, (1, 128), 1)
    key_at = lax.broadcasted_iota(jnp.int32, (1, n), 1)
    mask = jnp.where(key_at % padded >= rows, MASKED, 0.0).astype(F32)

    tile_f = 128

    def attend_pair(p, carry):
        for k, do in enumerate(((forward_y, 0), (forward_y, 1), (forward_y, 2), (forward_y, 3))):
            pl.when(p == k)(functools.partial(*do))
        pl.when(p == 3)(functools.partial(forward_x, 0))

        def attend_tile(i, carry):
            at = pl.ds(pl.multiple_of(i * tile_f, tile_f), tile_f)
            q = qkv[p, at, 0:128]
            outs, inverses = [], []
            for h in range(2):
                qm = jnp.where((lane // 64) == h, q, jnp.zeros_like(q))
                s = mm(qm, qkv[p, :, 128:256], 1, 1) + mask
                e = jnp.exp(s - jnp.max(s, axis=1, keepdims=True)).astype(BF16)
                prob[2 * p + h, at, :] = e
                o = mm(e, qkv[p, :, 256:512])
                outs.append(o[:, :128])
                inverses.append(1.0 / o[:, 128:])
            inverse = jnp.where(lane < 64, inverses[0], inverses[1])
            o = jnp.where(lane < 64, outs[0], outs[1]) * inverse
            lanes = pl.ds(pl.multiple_of(p * 128, 128), 128)
            mxf[at, lanes] = o
            mx[at, lanes] = o.astype(BF16)
            rinv[at, lanes] = inverse.astype(BF16)
            return carry

        lax.fori_loop(0, n // tile_f, attend_tile, 0, unroll=True)
        return carry

    lax.fori_loop(0, pairs, attend_pair, 0)
    forward_x(1)
    forward_x(2)

    load_wo.wait()

    def first_norm(i, carry):
        at = pl.ds(pl.multiple_of(i * padded, padded), padded)
        zz = en[at, :] + (mm(mx[at, :], wo[...]) + vec[OUT:OUT + 1, :])
        centred = zz - row_mean(zz)
        inv = lax.rsqrt(row_mean(centred * centred) + EPSILON)
        nn = centred * inv
        en[at, :] = nn
        inv1[at, :] = jnp.broadcast_to(inv, (padded, 128))
        out = nn * vec[GAIN1:GAIN1 + 1, :] + vec[SHIFT1:SHIFT1 + 1, :]
        flow[at, :] = out.astype(BF16)
        g2[at, :] = out + vec[DOWN:DOWN + 1, :]
        return carry

    lax.fori_loop(0, blocks, first_norm, 0)
    forward_x(3)

    tile_h = n // 2

    def feed_forward(j):
        for i in range(n // tile_h):
            at = slice(i * tile_h, (i + 1) * tile_h)
            v = mm(flow[at, :], wb[0, j], 1, 1) + ubb[j, 0:1, :]
            v2 = v * v
            half = 0.5 * jnp.tanh(v * (GELU_A + GELU_B * v2)) + 0.5
            h = v * half
            slope[j, at, :] = (
                half + h * (1.0 - half) * (2 * GELU_A + (6 * GELU_B) * v2)
            ).astype(BF16)
            h = h.astype(BF16)
            hid[j, at, :] = h
            g2[at, :] += mm(h, wb[1, j])

    for cp in own_w:
        cp.wait()
    feed_forward(t)
    for cp in stage_core + stage_ub:
        cp.wait()
    feed_forward(t_c)
    for cp in stage_x + stage_y:
        cp.wait_send()
    feed_forward(t_y)
    for cp in stage_d + stage_e:
        cp.wait()
    feed_forward(t_d)

    own_cot.wait()
    for cp in send_cot:
        cp.wait()

    def add_row(row, value, at=slice(None)):
        i = look + row
        gs[i // 64, (i // 16) % 4, i % 16:i % 16 + 1, at] += value

    gs[...] = jnp.zeros_like(gs)

    def second_norm(i, carry):
        at = pl.ds(pl.multiple_of(i * padded, padded), padded)
        acc = g2[at, :]
        centred = acc - row_mean(acc)
        inv = lax.rsqrt(row_mean(centred * centred) + EPSILON)
        nn = centred * inv
        up = pad_rows(cot[i].astype(F32), padded)
        result = nn * vec[GAIN2:GAIN2 + 1, :] + vec[SHIFT2:SHIFT2 + 1, :]
        cot[i] = result[:rows].astype(BF16)
        gg = up * vec[GAIN2:GAIN2 + 1, :]
        back = inv * (gg - row_mean(gg) - nn * row_mean(gg * nn))
        g2[at, :] = back
        low = back.astype(BF16)
        gb[at, :] = low
        add_row(S_GAIN2, col_sum(up * nn))
        add_row(S_SHIFT2, col_sum(up))
        add_row(S_DOWN, col_sum(low.astype(F32)))
        return carry

    lax.fori_loop(0, blocks, second_norm, 0)
    own_mixed = sems.local(cot.at[t], o_mixed.at[t])
    own_mixed.start()
    send_mixed = exchange(cot, o_mixed, lambda r: r.at[t])

    def add_into(dst, src, index):
        dst[index] = (dst[index].astype(F32) + src[...].astype(F32)).astype(dst.dtype)

    class FeedSum:
        def __init__(self, m, out):
            self.m, self.out = m, out
            self.flight = {}

        def start(self, key, src, dst, device):
            cp = sems.copy(src, dst, device)
            cp.start()
            self.flight.setdefault(key, []).append(cp)

        def wait(self, key):
            for cp in self.flight.pop(key):
                cp.wait()

        def ready(self, k):
            m = self.m
            if k < 2:
                self.start(("core", k), g.at[m, k], rc.at[m, k], core_dev)
                return
            self.wait(("core", k - 2))
            for h in range(2):
                for bb in range(2):
                    for zz in range(nz):
                        add_into(g, rc.at[m, k - 2, h, bb, zz], (m, k, h, bb, zz))
            if k == 2:
                self.start("y0", g.at[m, 2, 0], r1y.at[m], y_dev)
            self.start("x1", g.at[m, k, 1, bo], r1x.at[m, k - 2], x_dev)

        def second(self, h):
            m = self.m
            if h == 0:
                self.wait("y0")
                for bb in range(2):
                    for zz in range(nz):
                        add_into(g, r1y.at[m, bb, zz], (m, 3, 0, bb, zz))
                self.start("x0", g.at[m, 3, 0, bo], r2.at[m, 0], x_dev)
            else:
                self.wait("x1")
                for k in range(2):
                    for zz in range(nz):
                        add_into(g, r1x.at[m, k, zz], (m, 2 + k, 1, b, zz))
                self.start("y1", g.at[m, 2, 1, b], r2.at[m, 1], y_dev)

        def third(self, h):
            m = self.m
            self.wait("x0" if h == 0 else "y1")
            for zz in range(nz):
                add_into(g, r2.at[m, h, zz], (m, 3, h, b, zz))
            for k in range(1, nz):
                zz = (z + k) % nz
                self.start(
                    ("z", h), g.at[m, 3, h, b, zz], rz.at[m, h, k - 1], dev(c, y, b, zz)
                )

        def last(self, h):
            m = self.m
            self.wait(("z", h))
            total = g[m, 3, h, b, z].astype(F32)
            for k in range(nz - 1):
                total = total + rz[m, h, k].astype(F32)
            self.out[:, h * lanes2:(h + 1) * lanes2] = total

    class WholeSum:
        def __init__(self, grad, rcv, rcv1, rcvz, out):
            self.refs = (grad, rcv, rcv1, rcvz, out)

        def start(self, src, dst, device):
            cp = sems.copy(src, dst, device)
            cp.start()
            self.cps.append(cp)

        def wait(self):
            for cp in self.cps:
                cp.wait()
            self.cps = []

        def steps(self):
            grad, rcv, rcv1, rcvz, out = self.refs
            self.cps = []
            self.start(grad.at[co], rcv, core_dev)
            yield
            self.wait()
            for i in range(4):
                add_into(grad, rcv.at[i], (c, i))
            for k, (py, pb) in enumerate(xy_peers):
                self.start(grad.at[c, py * 2 + pb], rcv1.at[k], dev(c, py, pb))
            yield
            self.wait()
            total = grad[c, xy].astype(F32)
            for k in range(3):
                total = total + rcv1[k].astype(F32)
            rcvz[z] = total.astype(grad.dtype)
            for k in range(1, nz):
                self.start(rcvz.at[z], rcvz.at[z], dev(c, y, b, (z + k) % nz))
            yield
            self.wait()
            total = rcvz[0].astype(F32)
            for k in range(1, nz):
                total = total + rcvz[k].astype(F32)
            out[c, xy] = total.astype(grad.dtype)
            for py, pb in xy_peers:
                self.start(out.at[c, xy], out.at[c, xy], dev(c, py, pb))
            yield
            self.wait()
            self.start(out.at[c], out.at[c], core_dev)
            yield
            self.wait()

    down_sum, up_sum = FeedSum(0, o_down), FeedSum(1, o_up)
    order = (t_d, t_c, t_y, t)

    def feed_grad(m, k, left, right):
        out = mm(left, right, 0, 0).astype(BF16)
        for h in range(2):
            for zz in range(nz):
                for bb in range(2):
                    i = (zz * 2 + bb) * fr
                    g[m, k, h, bb, zz] = out[i:i + fr, h * lanes2:(h + 1) * lanes2]

    for k, j in enumerate(order):
        feed_grad(0, k, gb[...], hid[j])
        down_sum.ready(k)
    for cp in send_mixed[:2]:
        cp.start()

    def feed_back(k, j):
        for i in range(n // tile_h):
            at = slice(i * tile_h, (i + 1) * tile_h)
            gp = (slope[j, at, :].astype(F32) * mm(gb[at, :], wb[1, j], 1, 1)).astype(BF16)
            slope[j, at, :] = gp
            g2[at, :] += mm(gp, wb[0, j])
        up_rows[k] = col_sum(slope[j].astype(F32))
        feed_grad(1, k, flow[...], slope[j])

    up_rows = [None] * blocks
    for k, j in enumerate(order):
        feed_back(k, j)
        up_sum.ready(k)
        if k == 1:
            down_sum.second(0)
            down_sum.second(1)
        if k == 3:
            down_sum.third(0)
            down_sum.third(1)
    for k, j in enumerate(order):
        i = look + S_UP + j
        gs[i // 64, (i // 16) % 4, pl.ds(i % 16, 1), :] = up_rows[k]
    for cp in send_mixed[2:]:
        cp.start()

    def first_back(i, carry):
        at = pl.ds(pl.multiple_of(i * padded, padded), padded)
        acc = g2[at, :]
        nn = en[at, :]
        add_row(S_GAIN1, col_sum(acc * nn))
        add_row(S_SHIFT1, col_sum(acc))
        gg = acc * vec[GAIN1:GAIN1 + 1, :]
        inv = inv1[at, 0:1]
        back = inv * (gg - row_mean(gg) - nn * row_mean(gg * nn))
        ga = back.astype(BF16)
        hid[0, at, :] = ga
        gm = mm(ga, wo[...], 1, 1)
        gb[at, :] = (gm * rinv[at, :].astype(F32)).astype(BF16)
        return carry

    lax.fori_loop(0, blocks, first_back, 0)

    ga = hid.at[0]
    out_grad = mm(mx[...], ga[...], 0, 0).astype(BF16)
    for i in range(8):
        r = width // 8
        go[i // 4, i % 4] = out_grad[i * r:(i + 1) * r]
    out_steps = WholeSum(go, gorc, gor1, gorz, o_out).steps()
    next(out_steps)
    small = mm(xa[:, 0:128], ga[...], 0, 0)
    for i in range(8):
        gs[i // 4, i % 4] += small[16 * i:16 * i + 16]
    small_steps = WholeSum(gs, gsrc, gsr1, gsrz, o_small).steps()
    next(small_steps)

    tile_b = n // 2
    pair_steps = []

    def attend_back(p, between):
        lanes = pl.ds(p * 128, 128)
        qt[...] = qkv[p, :, 0:128].T
        dt[...] = gb[:, lanes].T
        for h in range(2):
            def tile(i, carry):
                at = pl.ds(pl.multiple_of(i * tile_b, tile_b), tile_b)
                d = gb[at, lanes]
                own = (lane // 64) == h
                dm = jnp.where(own, d, jnp.zeros_like(d))
                centre = jnp.sum(
                    jnp.where(own, d.astype(F32) * mxf[at, lanes], 0.0), axis=1, keepdims=True
                )
                s = (mm(dm, qkv[p, :, 256:384], 1, 1) - centre).astype(BF16)
                s = s * prob[2 * p + h, at, :]
                ds[at, :] = s
                dq = mm(s, qkv[p, :, 128:256])
                if h == 0:
                    mxf[at, lanes] = jnp.where(lane < 64, dq, mxf[at, lanes])
                else:
                    rinv[at, lanes] = jnp.where(lane < 64, mxf[at, lanes], dq).astype(BF16)
                return carry

            lax.fori_loop(0, n // tile_b, tile, 0, unroll=True)
            half = slice(64 * h, 64 * h + 64)
            dk = mm(qt[half, :], ds[...])
            dv = mm(dt[half, :], prob[2 * p + h])
            qt[half, :] = dk.astype(BF16)
            dt[half, :] = dv.astype(BF16)
            between[h]()
        qkv[p, :, 0:128] = rinv[:, lanes]
        qkv[p, :, 128:256] = qt[...].T
        qkv[p, :, 256:384] = dt[...].T
        grad = mm(xa[:, 0:128], qkv[p, :, 0:384], 0, 0).astype(BF16)
        for i in range(8):
            gp_[p, i // 4, i % 4] = grad[16 * i:16 * i + 16]
        steps = WholeSum(
            gp_.at[p], gprc.at[p], gpr1.at[p], gprz.at[p], o_pairs.at[p]
        ).steps()
        next(steps)
        pair_steps.append(steps)

    def advance(*steps):
        for s in steps:
            next(s, None)

    def at_0a():
        down_sum.last(0)
        down_sum.last(1)

    def at_0b():
        up_sum.second(0)
        up_sum.second(1)
        advance(out_steps, small_steps)

    def at_1a():
        pass

    def at_1b():
        up_sum.third(0)
        up_sum.third(1)
        advance(out_steps, small_steps, pair_steps[0])

    def at_2a():
        pass

    def at_2b():
        advance(out_steps, small_steps, pair_steps[0], pair_steps[1])

    def at_3a():
        advance(pair_steps[0])

    def at_3b():
        up_sum.last(0)
        up_sum.last(1)
        advance(out_steps, small_steps, pair_steps[1], pair_steps[2])

    attend_back(0, (at_0a, at_0b))
    attend_back(1, (at_1a, at_1b))
    attend_back(2, (at_2a, at_2b))
    attend_back(3, (at_3a, at_3b))

    out = mm(we[...], ga[...], 1, 1)
    for p in range(pairs):
        out = out + mm(w2[1 + p, 0:look, 0:384], qkv[p, :, 0:384], 1, 1)
    for i in range(blocks):
        xs[i, 0:look, :] = out[:, i * padded:i * padded + rows].astype(BF16)
    own_s = sems.local(xs.at[t, 0:look], o_series.at[t])
    own_s.start()
    send_s = []
    for k in range(1, blocks):
        other = (t + k) % blocks
        send_s.append(sems.copy(xs.at[other, 0:look], o_series.at[t], (dp, other)))
    for cp in send_s:
        cp.start()
    for _ in range(5):
        advance(*pair_steps, out_steps, small_steps)
    for cp in send_s + send_mixed:
        cp.wait()
    own_s.wait()
    own_mixed.wait()


def finish(cfg, *refs):
    pairs, n_in, n_out = cfg
    inputs, refs = refs[:n_in], refs[n_in:]
    results, refs = refs[:n_out], refs[n_out:]
    held, refs = refs[:n_in], refs[n_in:]
    made, (sem_in, sem_out) = refs[:-2], refs[-2:]
    mixed, sgrad, up, down, pair_sums, out, small, we, wq, wk, wv, be = held
    made = (mixed, sgrad, up, down) + tuple(made)
    loads = [
        pltpu.make_async_copy(src, dst, sem_in.at[i])
        for i, (src, dst) in enumerate(zip(inputs, held))
    ]
    stores = [
        pltpu.make_async_copy(src, dst, sem_out.at[i])
        for i, (src, dst) in enumerate(zip(made, results))
    ]
    o_q, o_k, o_v, o_o, o_we, o_be, o_bq, o_bv, o_bo, o_g1, o_s1, o_bu, o_bd, o_g2, o_s2 = made[4:]
    for i in (4, 7, 11, 8, 9, 10, 6, 5, 0, 1, 2, 3):
        loads[i].start()
    look, width = we.shape
    r = width // 8
    for i in (4, 7, 11):
        loads[i].wait()
    row = lax.broadcasted_iota(jnp.int32, (128, 1), 0)
    b_high = be[...].astype(BF16).astype(F32)
    left = pad_rows(we[...].astype(F32), 128)
    left = left + jnp.where(row == look, b_high, 0.0)
    left = (left + jnp.where(row == look + 1, be[...] - b_high, 0.0)).astype(BF16)
    total = jnp.zeros((128, width), F32)
    for j, (o, w) in enumerate(((o_q, wq), (o_k, wk), (o_v, wv))):
        sums = jnp.concatenate(
            [
                jnp.concatenate(
                    [pair_sums[p, i // 4, i % 4, :, 128 * j:128 * j + 128] for i in range(8)],
                    axis=0,
                ).astype(F32)
                for p in range(pairs)
            ],
            axis=1,
        )
        if j == 0:
            sums = sums * 0.125
        last = sums[look:look + 1]
        o[...] = mm(left, (sums + jnp.where(row == look + 1, last, 0.0)).astype(BF16), 0, 0)
        stores[4 + j].start()
        if j == 0:
            o_bq[...] = last
        if j == 2:
            o_bv[...] = last
        loads[8 + j].wait()
        total = total + mm(sums.astype(BF16), w[...], 1, 1)
    loads[6].wait()
    total = total + jnp.concatenate([small[i // 4, i % 4] for i in range(8)], axis=0)
    o_we[...] = total[:look]
    o_be[...] = total[look:look + 1]

    def vector(i):
        i = look + i
        return small[i // 64, (i // 16) % 4, i % 16:i % 16 + 1, :]

    o_bo[...] = vector(0)
    for o, i in (
        (o_g1, S_GAIN1), (o_s1, S_SHIFT1), (o_bd, S_DOWN), (o_g2, S_GAIN2), (o_s2, S_SHIFT2)
    ):
        o[...] = vector(i)
    for i in range(4):
        o_bu[:, i * width:(i + 1) * width] = vector(S_UP + i)
    for cp in stores[8:]:
        cp.start()
    loads[5].wait()
    for i in range(8):
        o_o[i * r:(i + 1) * r, :] = out[i // 4, i % 4].astype(F32)
    stores[7].start()
    for i in range(4):
        loads[i].wait()
        stores[i].start()
    for cp in stores:
        cp.wait()


def body(
    series, embed_weight, embed_bias, query_weight, query_bias, key_weight, value_weight,
    value_bias, out_weight, out_bias, first_gain, first_shift, up_weight, up_bias,
    down_weight, down_bias, second_gain, second_shift, cotangent,
    *, dp_size, tensor_size,
):
    windows, rows, look = series.shape
    width = embed_weight.shape[1]
    hidden = up_weight.shape[0]
    pairs = HEADS // 2
    assert windows == tensor_size == 4 and width == hidden == HEADS * 64
    assert dp_size % 2 == 0 and look % 16 == 0 and look + S_UP + 4 <= 128
    padded = -(-rows // 32) * 32
    n = tensor_size * padded
    nz = dp_size // 2
    fr = width // dp_size
    r = width // 8
    half = hidden // 2

    def scr(*shape, dtype=BF16):
        return pltpu.VMEM(shape, dtype)

    scratch = [
        scr(4, 128, rows),
        scr(n, 256),
        scr(n, width, dtype=F32),
        scr(pairs, n, 512),
        scr(HEADS, n, n),
        scr(n, n),
        scr(n, width, dtype=F32),
        scr(n, width),
        scr(n, width),
        scr(n, 128, dtype=F32),
        scr(n, width),
        scr(4, n, hidden),
        scr(4, n, hidden),
        scr(4, rows, width),
        scr(n, width, dtype=F32),
        scr(n, width),
        scr(128, n),
        scr(128, n),
        scr(2, 4, hidden, width),
        scr(pairs, width, 384),
        scr(width, width),
        scr(look, width),
        scr(1 + pairs, 256, width),
        scr(4, 8, hidden, dtype=F32),
        scr(2, 4, 2, 2, nz, fr, half),
        scr(2, 2, 2, 2, nz, fr, half),
        scr(2, 2, nz, fr, half),
        scr(2, 2, nz, fr, half),
        scr(2, 2, nz, fr, half),
        scr(2, 2, nz - 1, fr, half),
        scr(pairs, 2, 4, 16, 384),
        scr(pairs, 4, 16, 384),
        scr(pairs, 3, 16, 384),
        scr(pairs, nz, 16, 384),
        scr(2, 4, r, width),
        scr(4, r, width),
        scr(3, r, width),
        scr(nz, r, width),
        scr(2, 4, 16, width, dtype=F32),
        scr(4, 16, width, dtype=F32),
        scr(3, 16, width, dtype=F32),
        scr(nz, 16, width, dtype=F32),
        scr(16, width, dtype=F32),
        scr(8, hidden, dtype=F32),
        pltpu.SemaphoreType.DMA((N_SEMS + 16 * nz,)),
        pltpu.SemaphoreType.DMA((N_SEMS + 16 * nz,)),
    ]
    hbm = pl.BlockSpec(memory_space=pl.ANY)
    vmem = pl.BlockSpec(memory_space=pltpu.VMEM)
    sd = jax.ShapeDtypeStruct
    bias = embed_bias.reshape(1, -1)
    mixed, sgrad, g_pairs, g_out, g_small, g_up, g_down = pl.pallas_call(
        functools.partial(kernel, (4, rows, padded, nz, fr)),
        out_shape=[
            sd((4, rows, width), BF16),
            sd((4, look, rows), BF16),
            sd((pairs, 2, 4, 16, 384), BF16),
            sd((2, 4, r, width), BF16),
            sd((2, 4, 16, width), F32),
            sd((fr, hidden), F32),
            sd((fr, hidden), F32),
        ],
        in_specs=[hbm] * 9 + [vmem] * 10,
        out_specs=[hbm] * 2 + [vmem] * 5,
        scratch_shapes=scratch,
        compiler_params=pltpu.CompilerParams(
            collective_id=1, has_side_effects=True, vmem_limit_bytes=64 * 1024 * 1024
        ),
    )(
        jnp.swapaxes(series, 1, 2), cotangent, embed_weight, query_weight, key_weight,
        value_weight, out_weight, up_weight, down_weight, bias,
        *(v.reshape(1, -1) for v in (
            query_bias, value_bias, out_bias, first_gain, first_shift, down_bias,
            second_gain, second_shift, up_bias,
        )),
    )
    vector = sd((1, width), F32)
    operands = (
        mixed, sgrad, g_up, g_down, g_pairs, g_out, g_small, embed_weight, query_weight,
        key_weight, value_weight, bias,
    )
    made = [
        *[sd((width, width), F32)] * 4,
        sd((look, width), F32),
        *[vector] * 6,
        sd((1, 4 * hidden), F32),
        *[vector] * 3,
    ]
    out = pl.pallas_call(
        functools.partial(finish, (pairs, len(operands), 4 + len(made))),
        out_shape=[sd(a.shape, a.dtype) for a in operands[:4]] + made,
        in_specs=[hbm] * len(operands),
        out_specs=[hbm] * (4 + len(made)),
        scratch_shapes=[
            *[scr(*a.shape, dtype=a.dtype) for a in operands],
            *[scr(*a.shape, dtype=a.dtype) for a in made],
            pltpu.SemaphoreType.DMA((len(operands),)),
            pltpu.SemaphoreType.DMA((4 + len(made),)),
        ],
        compiler_params=pltpu.CompilerParams(vmem_limit_bytes=64 * 1024 * 1024),
    )(*operands)
    mixed, sgrad, g_up, g_down, g_q, g_k, g_v, g_o, g_e = out[:9]
    g_be, g_bq, g_bv, g_bo, g_g1, g_s1, g_bu, g_bd, g_g2, g_s2 = (
        v.reshape(-1) for v in out[9:]
    )
    return (
        mixed, jnp.swapaxes(sgrad, 1, 2), g_e, g_be, g_q, g_bq, g_k, g_v, g_bv, g_o, g_bo,
        g_g1, g_s1, g_up.T, g_bu, g_down.T, g_bd, g_g2, g_s2,
    )


def solution(mesh):
    token = P("dp", "tensor", None)
    return jax.shard_map(
        functools.partial(
            body, dp_size=mesh.shape["dp"], tensor_size=mesh.shape["tensor"]
        ),
        mesh=mesh,
        in_specs=(
            token, P(), P(), P(), P(), P(), P(), P(), P(), P(), P(), P(),
            P("tensor", None), P("tensor"), P("tensor", None), P(), P(), P(), token,
        ),
        out_specs=(
            token, token, P(), P(), P(), P(), P(), P(), P(), P(), P(), P(), P(),
            P("tensor", "dp"), P(), P("tensor", "dp"), P(), P(), P(),
        ),
        check_vma=False,
    )
```

time: 179 us -> 116 us (0.65)
  local copies, waits for them, and re-layouts: 31.7 us -> 1.25 us
  Pallas kernels: 143 us -> 114 us
  other arithmetic: 3.07 us -> 0 us
    pallas_call x1, Pallas kernels: 143 us -> 110 us  [body(): pl.pallas_call(functools.partial(kernel, (4, rows, padded, nz, fr)), out_...]
    slice x6 -> x0, local copies, waits for them, and re-layouts: 13.5 us -> none  [the longest x2 9.18 us: body(): g_qkv[2]]
    unnamed x20 -> x2, local copies, waits for them, and re-layouts: 9.34 us -> 0.67 us
    transpose x1 -> x0, local copies, waits for them, and re-layouts: 5.44 us -> none  [body(): g_qkv = g_qkv.transpose(2, 1, 0, 3).reshape(3, width, width)]
    pallas_call x0 -> x1, Pallas kernels: none -> 4.43 us  [body(): pl.pallas_call(functools.partial(finish, (pairs, len(operands), 4 + len(m...]
    convert_element_type x2 -> x0, other arithmetic: 3.07 us -> none  [the longest x1 2.14 us: body(): g_out.reshape(width, width).astype(F32)]
where the time goes in v2:
time: 116 us
  Pallas kernels  114 us (98%)
  local copies, waits for them, and re-layouts  1.25 us (1%)
    pallas_call x1, Pallas kernels, body(): pl.pallas_call(functools.partial(kernel, (4, rows, padded, nz, fr)), out_...  110 us
    pallas_call x1, Pallas kernels, body(): pl.pallas_call(functools.partial(finish, (pairs, len(operands), 4 + len(m...  4.43 us

profile of v2, /device:TPU:0, one launch (start us, length us, event | category | flops | bytes accessed | tf_op | source)
XLA Modules:
  0.0 116.2 jit_solution(17571293201063702738)
XLA Ops:
  0.7 0.0 copy-start
  0.7 0.7 copy-done
  1.3 0.6 reshape.107.b_up
  1.9 109.6 %shard_map.330 = (bf16[4,216,512]{2,1,0:T(8,128)(2,1)}, bf16[4,96,216]{2,1,0:T(8,128)(2,1)}, bf16[4,2,4,16,384]{4,3,2,1,0:T(8,128)(2,1)}, bf16[2,4,64,512]{3,2,1...) custom-call(bf16[4,96,216]{2,1,0:T(8,128)(2,1)} %bitcast.23, ...), custom_call_target="tpu_custom_call" | custom-call | tf_op jit(solution)/shard_map/pallas_call | solution.py:784
  111.5 4.4 %shard_map.331 = (bf16[4,216,512]{2,1,0:T(8,128)(2,1)}, bf16[4,96,216]{2,1,0:T(8,128)(2,1)}, f32[64,512]{1,0:T(8,128)}, f32[64,512]{1,0:T(8,128)}, f32[512,512]{...) custom-call(bf16[4,216,512]{2,1,0:T(8,128)(2,1)} %get-tuple-element., ...), custom_call_target="tpu_custom_call" | custom-call | tf_op jit(solution)/shard_map/pallas_call | solution.py:821
Async XLA Ops:
  0.7 0.7 copy-start

commit v3 on v2

--- a/solution.py
+++ b/solution.py
@@ -39,48 +39,97 @@
     return jnp.concatenate([x, jnp.zeros((rows - x.shape[0], x.shape[1]), x.dtype)], axis=0)
 
 
+class Copy:
+    def __init__(self, sems, make):
+        self.sems, self.make, self.copy = sems, make, None
+
+    def reserve(self):
+        self.slot = self.sems.take()
+        self.copy = self.make(self.sems.send.at[self.slot])
+
+    def start(self):
+        if self.copy is None:
+            self.reserve()
+        self.copy.start()
+
+    def wait_recv(self):
+        self.copy.wait_recv()
+
+    def wait_send(self):
+        self.copy.wait_send()
+        self.sems.free.append(self.slot)
+
+    def wait(self):
+        self.copy.wait()
+        self.sems.free.append(self.slot)
+
+
 class Sems:
     def __init__(self, send, recv):
-        self.send, self.recv, self.used = send, recv, 0
+        self.send, self.recv = send, recv
+        self.free = list(range(send.shape[0]))[::-1]
+        self.used = 0
+
+    def take(self):
+        return self.free.pop()
 
     def copy(self, src, dst, device):
         i = self.used
         self.used += 1
-        return pltpu.make_async_remote_copy(
+        assert i < self.recv.shape[0]
+        return Copy(self, lambda sem: pltpu.make_async_remote_copy(
             src_ref=src,
             dst_ref=dst,
-            send_sem=self.send.at[i],
+            send_sem=sem,
             recv_sem=self.recv.at[i],
             device_id=device,
             device_id_type=MESH,
-        )
+        ))
 
     def local(self, src, dst):
-        i = self.used
-        self.used += 1
-        return pltpu.make_async_copy(src, dst, self.send.at[i])
-
-    def slot(self):
-        i = self.used
-        self.used += 1
-        return self.send.at[i], self.recv.at[i]
-
-
-N_SEMS = 192
+        return Copy(self, lambda sem: pltpu.make_async_copy(src, dst, sem))
+
+
+N_SEND, N_SEND_Z = 44, 8
+N_RECV, N_RECV_Z = 96, 10
+
+AXES = {"d0": "xy", "d1": "yxz", "u0": "zxy", "u1": "zyx"}
+DIRECT = ("p3",)
+SCHEDULE = {
+    "dk3": ("m",),
+    "uk0": ("d0", "d0", "d1",),
+    "uk1": ("d1",),
+    "uk2": ("u0", "u1",),
+    "uk3": ("u0", "u1",),
+    "n1": ("d0",),
+    "a0b": ("S", "O", "d1",),
+    "a1a": ("u0", "d0", "p0", "m",),
+    "a1w": ("S",),
+    "a2a": ("p1", "u1",),
+    "a2b": ("O",),
+    "a3a": ("d0", "d1", "p2",),
+    "a3w": ("S",),
+    "sb": ("u0", "p1", "p0",),
+    "end": (
+        "u1", "p2", "O", "p3", "d1", "u1", "S", "p1", "u0", "S",
+        "p0", "p2", "p3", "O", "p1", "d1", "p0", "O", "p2", "p1",
+        "p0", "u1", "p2", "p3", "u0",
+    ),
+}
 
 
 def kernel(
     cfg,
     series, cot_in, w_embed, w_q, w_k, w_v, w_o, w_up, w_down,
     b_embed, b_query, b_value, b_out, gain1, shift1, b_down, gain2, shift2, b_up,
-    o_mixed, o_series, o_pairs, o_out, o_small, o_up, o_down,
+    o_mixed, o_series, h_pairs, h_out, h_small, h_up, h_down,
     xs, xa, en, qkv, prob, ds, mxf, mx, rinv, inv1, flow, hid, slope, cot, g2, gb,
     qt, dt, wb, wqkv, wo, we, w2, ubb,
-    g, rc, r1y, r1x, r2, rz,
+    g, rc, r1, r2, r3, rz,
     gp_, gprc, gpr1, gprz,
     go, gorc, gor1, gorz,
     gs, gsrc, gsr1, gsrz,
-    vec, ubl, send, recv,
+    o_pairs, o_out, o_small, o_up, o_down, vec, upv, ubl, send, recv,
 ):
     blocks, rows, padded, nz, fr = cfg
     n = blocks * padded
@@ -103,8 +152,8 @@
     xy_peers = [(y, bo), (yo, b), (yo, bo)]
 
     barrier = pltpu.get_barrier_semaphore()
-    partners = [dev(co, y, b), dev(co, yo, b)]
-    partners += [dev(c, py, pb) for py, pb in xy_peers]
+    partners = [core_dev]
+    partners += [dev(cc, py, pb) for cc in (c, co) for py, pb in xy_peers]
     partners += [dev(c, y, b, (z + k) % nz) for k in range(1, nz)]
     for partner in partners:
         pl.semaphore_signal(barrier, inc=1, device_id=partner, device_id_type=MESH)
@@ -114,6 +163,11 @@
         cp.start()
         return cp
 
+    load_vec = [load(b_up, upv)]
+    for i, ref in enumerate(
+        (b_embed, b_query, b_value, b_out, gain1, shift1, b_down, gain2, shift2)
+    ):
+        load_vec.append(load(ref, vec.at[i]))
     load_we = load(w_embed, we)
     load_qkv = []
     for p in range(pairs):
@@ -125,11 +179,9 @@
     own_w = [load(w, wb.at[m, t]) for m, w in enumerate((w_up, w_down))]
     load_wo = load(w_o, wo)
     own_cot = load(cot_in.at[t], cot.at[t])
-    for i, ref in enumerate(
-        (b_embed, b_query, b_value, b_out, gain1, shift1, b_down, gain2, shift2)
-    ):
-        vec[i:i + 1, :] = ref[...]
-    ubl[...] = jnp.broadcast_to(b_up[...].astype(F32), ubl.shape)
+    for cp in load_vec:
+        cp.wait()
+    ubl[...] = jnp.broadcast_to(upv[...].astype(F32), ubl.shape)
     ubb[t] = ubl[...]
     tail_rows = xs.shape[1] - look
     first = lax.broadcasted_iota(jnp.int32, (tail_rows, rows), 0) == 0
@@ -166,6 +218,9 @@
     for cp in send_x + stage_ub + stage_y + stage_core + send_cot:
         cp.start()
 
+    for cp in stage_x + stage_d + stage_e:
+        cp.reserve()
+
     def forward_y(i):
         stage_y[i].wait_recv()
         stage_x[i].start()
@@ -177,8 +232,8 @@
 
     load_we.wait()
     one_row = lax.broadcasted_iota(jnp.int32, (128, 1), 0)
-    b_high = vec[EMBED:EMBED + 1, :].astype(BF16)
-    b_low = vec[EMBED:EMBED + 1, :] - b_high.astype(F32)
+    b_high = vec[EMBED].astype(BF16)
+    b_low = vec[EMBED] - b_high.astype(F32)
     we_rows = pad_rows(we[...].astype(F32), 128)
     high = we_rows + jnp.where(one_row == look, b_high.astype(F32), 0.0)
     low = jnp.where(one_row == look, b_low, 0.0)
@@ -192,7 +247,7 @@
         prod = mm(both, wqkv[p])
         bias = prod[look:look + 1] + prod[look + 1:look + 2]
         bias = bias + jnp.concatenate(
-            [vec[QUERY:QUERY + 1, at], jnp.zeros((1, 128), F32), vec[VALUE:VALUE + 1, at]],
+            [vec[QUERY, :, at], jnp.zeros((1, 128), F32), vec[VALUE, :, at]],
             axis=1,
         )
         prod = jnp.where(one_row < look, prod, jnp.where(one_row == look, bias, 0.0))
@@ -261,15 +316,15 @@
 
     def first_norm(i, carry):
         at = pl.ds(pl.multiple_of(i * padded, padded), padded)
-        zz = en[at, :] + (mm(mx[at, :], wo[...]) + vec[OUT:OUT + 1, :])
+        zz = en[at, :] + (mm(mx[at, :], wo[...]) + vec[OUT])
         centred = zz - row_mean(zz)
         inv = lax.rsqrt(row_mean(centred * centred) + EPSILON)
         nn = centred * inv
         en[at, :] = nn
         inv1[at, :] = jnp.broadcast_to(inv, (padded, 128))
-        out = nn * vec[GAIN1:GAIN1 + 1, :] + vec[SHIFT1:SHIFT1 + 1, :]
+        out = nn * vec[GAIN1] + vec[SHIFT1]
         flow[at, :] = out.astype(BF16)
-        g2[at, :] = out + vec[DOWN:DOWN + 1, :]
+        g2[at, :] = out + vec[DOWN]
         return carry
 
     lax.fori_loop(0, blocks, first_norm, 0)
@@ -321,9 +376,9 @@
         inv = lax.rsqrt(row_mean(centred * centred) + EPSILON)
         nn = centred * inv
         up = pad_rows(cot[i].astype(F32), padded)
-        result = nn * vec[GAIN2:GAIN2 + 1, :] + vec[SHIFT2:SHIFT2 + 1, :]
+        result = nn * vec[GAIN2] + vec[SHIFT2]
         cot[i] = result[:rows].astype(BF16)
-        gg = up * vec[GAIN2:GAIN2 + 1, :]
+        gg = up * vec[GAIN2]
         back = inv * (gg - row_mean(gg) - nn * row_mean(gg * nn))
         g2[at, :] = back
         low = back.astype(BF16)
@@ -336,77 +391,18 @@
     lax.fori_loop(0, blocks, second_norm, 0)
     own_mixed = sems.local(cot.at[t], o_mixed.at[t])
     own_mixed.start()
-    send_mixed = exchange(cot, o_mixed, lambda r: r.at[t])
+    send_mixed = [
+        sems.copy(cot.at[other], o_mixed.at[t], (dp, other)) for other in (t_c, t_y, t_d)
+    ]
+    send_mixed[0].start()
+    send_mixed_y = send_mixed[1:]
 
     def add_into(dst, src, index):
         dst[index] = (dst[index].astype(F32) + src[...].astype(F32)).astype(dst.dtype)
 
-    class FeedSum:
-        def __init__(self, m, out):
-            self.m, self.out = m, out
-            self.flight = {}
-
-        def start(self, key, src, dst, device):
-            cp = sems.copy(src, dst, device)
-            cp.start()
-            self.flight.setdefault(key, []).append(cp)
-
-        def wait(self, key):
-            for cp in self.flight.pop(key):
-                cp.wait()
-
-        def ready(self, k):
-            m = self.m
-            if k < 2:
-                self.start(("core", k), g.at[m, k], rc.at[m, k], core_dev)
-                return
-            self.wait(("core", k - 2))
-            for h in range(2):
-                for bb in range(2):
-                    for zz in range(nz):
-                        add_into(g, rc.at[m, k - 2, h, bb, zz], (m, k, h, bb, zz))
-            if k == 2:
-                self.start("y0", g.at[m, 2, 0], r1y.at[m], y_dev)
-            self.start("x1", g.at[m, k, 1, bo], r1x.at[m, k - 2], x_dev)
-
-        def second(self, h):
-            m = self.m
-            if h == 0:
-                self.wait("y0")
-                for bb in range(2):
-                    for zz in range(nz):
-                        add_into(g, r1y.at[m, bb, zz], (m, 3, 0, bb, zz))
-                self.start("x0", g.at[m, 3, 0, bo], r2.at[m, 0], x_dev)
-            else:
-                self.wait("x1")
-                for k in range(2):
-                    for zz in range(nz):
-                        add_into(g, r1x.at[m, k, zz], (m, 2 + k, 1, b, zz))
-                self.start("y1", g.at[m, 2, 1, b], r2.at[m, 1], y_dev)
-
-        def third(self, h):
-            m = self.m
-            self.wait("x0" if h == 0 else "y1")
-            for zz in range(nz):
-                add_into(g, r2.at[m, h, zz], (m, 3, h, b, zz))
-            for k in range(1, nz):
-                zz = (z + k) % nz
-                self.start(
-                    ("z", h), g.at[m, 3, h, b, zz], rz.at[m, h, k - 1], dev(c, y, b, zz)
-                )
-
-        def last(self, h):
-            m = self.m
-            self.wait(("z", h))
-            total = g[m, 3, h, b, z].astype(F32)
-            for k in range(nz - 1):
-                total = total + rz[m, h, k].astype(F32)
-            self.out[:, h * lanes2:(h + 1) * lanes2] = total
-
-    class WholeSum:
-        def __init__(self, grad, rcv, rcv1, rcvz, out):
-            self.refs = (grad, rcv, rcv1, rcvz, out)
-
+    results = []
+
+    class Sum:
         def start(self, src, dst, device):
             cp = sems.copy(src, dst, device)
             cp.start()
@@ -417,14 +413,111 @@
                 cp.wait()
             self.cps = []
 
+    def free_axes(order):
+        axes = [a for a in order if a != "y"]
+        return axes if "z" in axes else axes + ["z"]
+
+    mine, theirs = {"x": b, "z": z % 2}, {"x": bo, "z": 1 - z % 2}
+    z_near = z + 1 - 2 * (z % 2)
+    axis_dev = {"y": y_dev, "x": x_dev, "z": dev(c, y, b, z_near)}
+
+    class FeedSum(Sum):
+        def __init__(self, m, h, axes, out):
+            self.m, self.h, self.axes, self.out = m, h, axes, out
+            self.free = free_axes(axes)
+            self.core = []
+            self.cps = []
+
+        def at(self, *index):
+            return (self.m, self.h) + index
+
+        def send_core(self, k):
+            cp = sems.copy(g.at[self.at(k)], rc.at[self.at(k)], core_dev)
+            cp.start()
+            self.core.append(cp)
+
+        def add_core(self, k):
+            self.core[k - 2].wait()
+            add_into(g, rc.at[self.at(k - 2)], self.at(k))
+
+        def send(self, axis, slices, fixed, to):
+            for i, k in enumerate(slices):
+                src = g.at[self.at(k, *fixed)]
+                dst = to
+                if axis != "y":
+                    src = g.at[self.at(k, *fixed, theirs[axis])]
+                    dst = to if len(slices) == 1 else to.at[i]
+                self.start(src, dst, axis_dev[axis])
+
+        def steps(self):
+            m, h = self.m, self.h
+            stages = [r1.at[m, h], r2.at[m, h], r3.at[m, h]]
+            axes, fixed, slices = self.axes, [], [2, 3]
+            self.add_core(2)
+            if axes[0] == "y":
+                self.send("y", [2], [], stages[0])
+            else:
+                self.start(
+                    g.at[self.at(2, theirs[axes[0]])], stages[0].at[0], axis_dev[axes[0]]
+                )
+            yield
+            self.add_core(3)
+            if axes[0] != "y":
+                self.start(
+                    g.at[self.at(3, theirs[axes[0]])], stages[0].at[1], axis_dev[axes[0]]
+                )
+            yield
+            for i, axis in enumerate(axes):
+                self.wait()
+                if axis == "y":
+                    slices = [3]
+                    add_into(g, stages[i], self.at(3, *fixed))
+                else:
+                    fixed = fixed + [mine[axis]]
+                    for j, k in enumerate(slices):
+                        got = stages[i] if len(slices) == 1 else stages[i].at[j]
+                        add_into(g, got, self.at(k, *fixed))
+                if i + 1 < len(axes):
+                    nxt = axes[i + 1]
+                    self.send(nxt, [2] if nxt == "y" else slices, fixed, stages[i + 1])
+                    yield
+            if "z" in axes:
+                far = [((z // 2 + k) % (nz // 2)) for k in range(1, nz // 2)]
+                parts = [(dev(c, y, b, f * 2 + z % 2), fixed + [f]) for f in far]
+                own = fixed + [z // 2]
+            else:
+                far = [(z + k) % nz for k in range(1, nz)]
+                parts = [(dev(c, y, b, f), fixed + [f % 2, f // 2]) for f in far]
+                own = fixed + [z % 2, z // 2]
+            for k, (to, at) in enumerate(parts):
+                self.start(g.at[self.at(3, *at)], rz.at[m, h, k], to)
+            yield
+            self.wait()
+            total = g[self.at(3, *own)].astype(F32)
+            for k in range(len(parts)):
+                total = total + rz[m, h, k].astype(F32)
+            at = (slice(None), slice(h * lanes2, (h + 1) * lanes2))
+            self.out[0][at] = total
+            results.append(load(self.out[0].at[at], self.out[1].at[at]))
+
+    class WholeSum(Sum):
+        def __init__(self, key, grad, rcv, rcv1, rcvz, out, result):
+            self.direct = key in DIRECT
+            self.refs = (grad, rcv, rcv1, rcvz, out)
+            self.result = result
+
         def steps(self):
             grad, rcv, rcv1, rcvz, out = self.refs
             self.cps = []
-            self.start(grad.at[co], rcv, core_dev)
-            yield
-            self.wait()
-            for i in range(4):
-                add_into(grad, rcv.at[i], (c, i))
+            if self.direct:
+                for k, (py, pb) in enumerate([(y, b)] + xy_peers):
+                    self.start(grad.at[co, py * 2 + pb], rcv.at[k], dev(co, py, pb))
+            else:
+                self.start(grad.at[co], rcv, core_dev)
+                yield
+                self.wait()
+                for i in range(4):
+                    add_into(grad, rcv.at[i], (c, i))
             for k, (py, pb) in enumerate(xy_peers):
                 self.start(grad.at[c, py * 2 + pb], rcv1.at[k], dev(c, py, pb))
             yield
@@ -432,6 +525,9 @@
             total = grad[c, xy].astype(F32)
             for k in range(3):
                 total = total + rcv1[k].astype(F32)
+            if self.direct:
+                for k in range(4):
+                    total = total + rcv[k].astype(F32)
             rcvz[z] = total.astype(grad.dtype)
             for k in range(1, nz):
                 self.start(rcvz.at[z], rcvz.at[z], dev(c, y, b, (z + k) % nz))
@@ -443,13 +539,33 @@
             out[c, xy] = total.astype(grad.dtype)
             for py, pb in xy_peers:
                 self.start(out.at[c, xy], out.at[c, xy], dev(c, py, pb))
+            if self.direct:
+                for py, pb in [(y, b)] + xy_peers:
+                    self.start(out.at[c, xy], out.at[c, xy], dev(co, py, pb))
+            else:
+                yield
+                self.wait()
+                self.start(out.at[c], out.at[c], core_dev)
             yield
             self.wait()
-            self.start(out.at[c], out.at[c], core_dev)
-            yield
-            self.wait()
-
-    down_sum, up_sum = FeedSum(0, o_down), FeedSum(1, o_up)
+            results.append(load(out, self.result))
+
+    chains = {}
+    feeds = {}
+    for m, (name, out) in enumerate((("d", (o_down, h_down)), ("u", (o_up, h_up)))):
+        for h in range(2):
+            key = name + str(h)
+            feeds[key] = FeedSum(m, h, AXES[key], out)
+
+    def point(name):
+        for key in SCHEDULE.get(name, ()):
+            if key == "m":
+                send_mixed_y.pop(0).start()
+            else:
+                if key not in chains:
+                    chains[key] = feeds[key].steps()
+                next(chains[key], None)
+
     order = (t_d, t_c, t_y, t)
 
     def feed_grad(m, k, left, right):
@@ -458,13 +574,18 @@
             for zz in range(nz):
                 for bb in range(2):
                     i = (zz * 2 + bb) * fr
-                    g[m, k, h, bb, zz] = out[i:i + fr, h * lanes2:(h + 1) * lanes2]
+                    at = {"x": bb, "z": zz % 2}
+                    at = tuple(at[a] for a in feeds["du"[m] + str(h)].free)
+                    g[(m, h, k) + at + (zz // 2,)] = out[i:i + fr, h * lanes2:(h + 1) * lanes2]
+
+    point("n2")
 
     for k, j in enumerate(order):
         feed_grad(0, k, gb[...], hid[j])
-        down_sum.ready(k)
-    for cp in send_mixed[:2]:
-        cp.start()
+        if k < 2:
+            feeds["d0"].send_core(k)
+            feeds["d1"].send_core(k)
+        point("dk" + str(k))
 
     def feed_back(k, j):
         for i in range(n // tile_h):
@@ -478,18 +599,13 @@
     up_rows = [None] * blocks
     for k, j in enumerate(order):
         feed_back(k, j)
-        up_sum.ready(k)
-        if k == 1:
-            down_sum.second(0)
-            down_sum.second(1)
-        if k == 3:
-            down_sum.third(0)
-            down_sum.third(1)
+        if k < 2:
+            feeds["u0"].send_core(k)
+            feeds["u1"].send_core(k)
+        point("uk" + str(k))
     for k, j in enumerate(order):
         i = look + S_UP + j
         gs[i // 64, (i // 16) % 4, pl.ds(i % 16, 1), :] = up_rows[k]
-    for cp in send_mixed[2:]:
-        cp.start()
 
     def first_back(i, carry):
         at = pl.ds(pl.multiple_of(i * padded, padded), padded)
@@ -497,7 +613,7 @@
         nn = en[at, :]
         add_row(S_GAIN1, col_sum(acc * nn))
         add_row(S_SHIFT1, col_sum(acc))
-        gg = acc * vec[GAIN1:GAIN1 + 1, :]
+        gg = acc * vec[GAIN1]
         inv = inv1[at, 0:1]
         back = inv * (gg - row_mean(gg) - nn * row_mean(gg * nn))
         ga = back.astype(BF16)
@@ -507,24 +623,25 @@
         return carry
 
     lax.fori_loop(0, blocks, first_back, 0)
+    point("n1")
 
     ga = hid.at[0]
     out_grad = mm(mx[...], ga[...], 0, 0).astype(BF16)
     for i in range(8):
         r = width // 8
         go[i // 4, i % 4] = out_grad[i * r:(i + 1) * r]
-    out_steps = WholeSum(go, gorc, gor1, gorz, o_out).steps()
-    next(out_steps)
+    chains["O"] = WholeSum("O", go, gorc, gor1, gorz, o_out, h_out).steps()
+    next(chains["O"])
     small = mm(xa[:, 0:128], ga[...], 0, 0)
     for i in range(8):
         gs[i // 4, i % 4] += small[16 * i:16 * i + 16]
-    small_steps = WholeSum(gs, gsrc, gsr1, gsrz, o_small).steps()
-    next(small_steps)
+    chains["S"] = WholeSum("S", gs, gsrc, gsr1, gsrz, o_small, h_small).steps()
+    next(chains["S"])
+    point("og")
 
     tile_b = n // 2
-    pair_steps = []
-
-    def attend_back(p, between):
+
+    def attend_back(p):
         lanes = pl.ds(p * 128, 128)
         qt[...] = qkv[p, :, 0:128].T
         dt[...] = gb[:, lanes].T
@@ -553,58 +670,24 @@
             dv = mm(dt[half, :], prob[2 * p + h])
             qt[half, :] = dk.astype(BF16)
             dt[half, :] = dv.astype(BF16)
-            between[h]()
+            point("a" + str(p) + "ab"[h])
         qkv[p, :, 0:128] = rinv[:, lanes]
         qkv[p, :, 128:256] = qt[...].T
         qkv[p, :, 256:384] = dt[...].T
         grad = mm(xa[:, 0:128], qkv[p, :, 0:384], 0, 0).astype(BF16)
         for i in range(8):
             gp_[p, i // 4, i % 4] = grad[16 * i:16 * i + 16]
-        steps = WholeSum(
-            gp_.at[p], gprc.at[p], gpr1.at[p], gprz.at[p], o_pairs.at[p]
+        key = "p" + str(p)
+        chains[key] = WholeSum(
+            key, gp_.at[p], gprc.at[p], gpr1.at[p], gprz.at[p], o_pairs.at[p], h_pairs.at[p]
         ).steps()
-        next(steps)
-        pair_steps.append(steps)
-
-    def advance(*steps):
-        for s in steps:
-            next(s, None)
-
-    def at_0a():
-        down_sum.last(0)
-        down_sum.last(1)
-
-    def at_0b():
-        up_sum.second(0)
-        up_sum.second(1)
-        advance(out_steps, small_steps)
-
-    def at_1a():
-        pass
-
-    def at_1b():
-        up_sum.third(0)
-        up_sum.third(1)
-        advance(out_steps, small_steps, pair_steps[0])
-
-    def at_2a():
-        pass
-
-    def at_2b():
-        advance(out_steps, small_steps, pair_steps[0], pair_steps[1])
-
-    def at_3a():
-        advance(pair_steps[0])
-
-    def at_3b():
-        up_sum.last(0)
-        up_sum.last(1)
-        advance(out_steps, small_steps, pair_steps[1], pair_steps[2])
-
-    attend_back(0, (at_0a, at_0b))
-    attend_back(1, (at_1a, at_1b))
-    attend_back(2, (at_2a, at_2b))
-    attend_back(3, (at_3a, at_3b))
+        next(chains[key])
+        point("a" + str(p) + "w")
+
+    attend_back(0)
+    attend_back(1)
+    attend_back(2)
+    attend_back(3)
 
     out = mm(we[...], ga[...], 1, 1)
     for p in range(pairs):
@@ -619,12 +702,17 @@
         send_s.append(sems.copy(xs.at[other, 0:look], o_series.at[t], (dp, other)))
     for cp in send_s:
         cp.start()
-    for _ in range(5):
-        advance(*pair_steps, out_steps, small_steps)
+    point("sb")
+    point("end")
+    while send_mixed_y:
+        send_mixed_y.pop(0).start()
+    for _ in range(6):
+        for key in chains:
+            next(chains[key], None)
     for cp in send_s + send_mixed:
         cp.wait()
-    own_s.wait()
-    own_mixed.wait()
+    for cp in results + [own_s, own_mixed]:
+        cp.wait()
 
 
 def finish(cfg, *refs):
@@ -718,7 +806,7 @@
     hidden = up_weight.shape[0]
     pairs = HEADS // 2
     assert windows == tensor_size == 4 and width == hidden == HEADS * 64
-    assert dp_size % 2 == 0 and look % 16 == 0 and look + S_UP + 4 <= 128
+    assert dp_size % 4 == 0 and look % 16 == 0 and look + S_UP + 4 <= 128
     padded = -(-rows // 32) * 32
     n = tensor_size * padded
     nz = dp_size // 2
@@ -754,11 +842,11 @@
         scr(look, width),
         scr(1 + pairs, 256, width),
         scr(4, 8, hidden, dtype=F32),
-        scr(2, 4, 2, 2, nz, fr, half),
-        scr(2, 2, 2, 2, nz, fr, half),
-        scr(2, 2, nz, fr, half),
-        scr(2, 2, nz, fr, half),
-        scr(2, 2, nz, fr, half),
+        scr(2, 2, 4, 2, 2, nz // 2, fr, half),
+        scr(2, 2, 2, 2, 2, nz // 2, fr, half),
+        scr(2, 2, 2, 2, nz // 2, fr, half),
+        scr(2, 2, 2, nz // 2, fr, half),
+        scr(2, 2, nz // 2, fr, half),
         scr(2, 2, nz - 1, fr, half),
         scr(pairs, 2, 4, 16, 384),
         scr(pairs, 4, 16, 384),
@@ -772,10 +860,16 @@
         scr(4, 16, width, dtype=F32),
         scr(3, 16, width, dtype=F32),
         scr(nz, 16, width, dtype=F32),
-        scr(16, width, dtype=F32),
+        scr(pairs, 2, 4, 16, 384),
+        scr(2, 4, r, width),
+        scr(2, 4, 16, width, dtype=F32),
+        scr(fr, hidden, dtype=F32),
+        scr(fr, hidden, dtype=F32),
+        scr(9, 1, width, dtype=F32),
+        scr(1, hidden),
         scr(8, hidden, dtype=F32),
-        pltpu.SemaphoreType.DMA((N_SEMS + 16 * nz,)),
-        pltpu.SemaphoreType.DMA((N_SEMS + 16 * nz,)),
+        pltpu.SemaphoreType.DMA((N_SEND + N_SEND_Z * nz,)),
+        pltpu.SemaphoreType.DMA((N_RECV + N_RECV_Z * nz,)),
     ]
     hbm = pl.BlockSpec(memory_space=pl.ANY)
     vmem = pl.BlockSpec(memory_space=pltpu.VMEM)
@@ -792,8 +886,8 @@
             sd((fr, hidden), F32),
             sd((fr, hidden), F32),
         ],
-        in_specs=[hbm] * 9 + [vmem] * 10,
-        out_specs=[hbm] * 2 + [vmem] * 5,
+        in_specs=[hbm] * 19,
+        out_specs=[hbm] * 7,
         scratch_shapes=scratch,
         compiler_params=pltpu.CompilerParams(
             collective_id=1, has_side_effects=True, vmem_limit_bytes=64 * 1024 * 1024

time: 116 us -> 88.9 us (0.77)
  Pallas kernels: 114 us -> 86.6 us
    pallas_call x1, Pallas kernels: 110 us -> 82.2 us  [body(): pl.pallas_call(functools.partial(kernel, (4, rows, padded, nz, fr)), out_...]
where the time goes in v3:
time: 88.9 us; the launch traced here: 88.7 us
  Pallas kernels  86.6 us (97%)
  local copies, waits for them, and re-layouts  1.25 us (1%)
    pallas_call x1, Pallas kernels, body(): pl.pallas_call(functools.partial(kernel, (4, rows, padded, nz, fr)), out_...  82.2 us
    pallas_call x1, Pallas kernels, body(): pl.pallas_call(functools.partial(finish, (pairs, len(operands), 4 + len(m...  4.43 us

profile of v3, /device:TPU:0, one launch (start us, length us, event | category | flops | bytes accessed | tf_op | source)
XLA Modules:
  0.0 88.7 jit_solution(2052560720414573276)
XLA Ops:
  0.7 0.0 copy-start
  0.7 0.7 copy-done
  1.3 0.6 reshape.107.b_up
  1.9 82.2 %shard_map.330 = (bf16[4,216,512]{2,1,0:T(8,128)(2,1)}, bf16[4,96,216]{2,1,0:T(8,128)(2,1)}, bf16[4,2,4,16,384]{4,3,2,1,0:T(8,128)(2,1)}, bf16[2,4,64,512]{3,2,1...) custom-call(bf16[4,96,216]{2,1,0:T(8,128)(2,1)} %bitcast.23, ...), custom_call_target="tpu_custom_call" | custom-call | tf_op jit(solution)/shard_map/pallas_call | solution.py:878
  84.1 4.4 %shard_map.331 = (bf16[4,216,512]{2,1,0:T(8,128)(2,1)}, bf16[4,96,216]{2,1,0:T(8,128)(2,1)}, f32[64,512]{1,0:T(8,128)}, f32[64,512]{1,0:T(8,128)}, f32[512,512]{...) custom-call(bf16[4,216,512]{2,1,0:T(8,128)(2,1)} %get-tuple-element., ...), custom_call_target="tpu_custom_call" | custom-call | tf_op jit(solution)/shard_map/pallas_call | solution.py:915
Async XLA Ops:
  0.7 0.7 copy-start
